TPU v7x, 32 devices: a whole 2x2x4 slice. The times are simulated.
32 devices in a mesh: lat: 4 (over x, core), lon: 8 (over z, y).
Axes of the slice: x: 2, y: 2, z: 4, core: 2. Of those that a mesh axis runs over, the one named last changes fastest.
Arguments:
- tokens: bfloat16 [2, 24, 96, 192], P(None, 'lat', 'lon'), may hold values from -6 to 6
- gain_one: float32 [192], replicated, may hold values from 0.1 to 1.9
- gain_two: float32 [192], replicated, may hold values from 0.1 to 1.9
- qkv_weight: bfloat16 [192, 576], replicated, may hold values from -0.4375 to 0.4375
- proj_weight: bfloat16 [192, 192], replicated, may hold values from -0.4375 to 0.4375
- up_weight: bfloat16 [192, 768], replicated, may hold values from -0.4375 to 0.4375
- down_weight: bfloat16 [768, 192], replicated, may hold values from -0.21875 to 0.21875
- bias_table: float32 [6, 1, 4, 3312], P(None, None, 'lat'), may hold values from -6 to 306
- pos_index: int32 [144, 144], replicated, may hold values from 0 to 3311
- mask_ids: int32 [2, 24, 96], P(None, 'lat', 'lon'), may hold values from 0 to 2
- cotangent: bfloat16 [2, 24, 96, 192], P(None, 'lat', 'lon'), may hold values from -6 to 6
Outputs:
- output: bfloat16 [2, 24, 96, 192], P(None, 'lat', 'lon')
- delta_tokens: bfloat16 [2, 24, 96, 192], P(None, 'lat', 'lon')
- grad_gain_one: float32 [192], replicated
- grad_gain_two: float32 [192], replicated
- grad_qkv: float32 [192, 576], replicated
- grad_proj: float32 [192, 192], replicated
- grad_up: float32 [192, 768], replicated
- grad_down: float32 [768, 192], replicated
- grad_bias: float32 [6, 1, 4, 3312], P(None, None, 'lat')
All inputs are finite; a program needn't handle non-finite values.
Results may differ from a plain program's by a relative error of at most 0.025.
Values may be sent and summed in bfloat16 or wider, within the bound.
A program may use at most 64 MiB of HBM per device.

v0:
```python
import math

import jax
import jax.numpy as jnp
from jax import lax
from jax.sharding import PartitionSpec as P

HEADS = 6
WZ = 2
WLAT = 6
WLON = 12
WT = 144
NPOS = 3312


EPS = 1e-05


def passed_along(x, axis, by):
    peers = lax.axis_size(axis)
    return lax.ppermute(x, axis, [(i, (i + by) % peers) for i in range(peers)])


def norm_stats(values):
    widened = values.astype(jnp.float32)
    center = widened - jnp.mean(widened, axis=-1, keepdims=True)
    spread = jnp.mean(center * center, axis=-1, keepdims=True)
    inverse = lax.rsqrt(spread + EPS)
    return (center * inverse, inverse)


def norm_back(delta_hidden, normal, inverse, gain):
    grad_gain = jnp.sum((delta_hidden * normal).reshape(-1, normal.shape[-1]), axis=0)
    delta_normal = delta_hidden * gain
    delta_input = inverse * (
        delta_normal
        - jnp.mean(delta_normal, axis=-1, keepdims=True)
        - normal * jnp.mean(delta_normal * normal, axis=-1, keepdims=True)
    )
    return (delta_input, grad_gain)


def gelu_pair(up_proj):
    cumulative = 0.5 * (1.0 + lax.erf(up_proj * 0.7071067811865476))
    density = jnp.exp(-0.5 * up_proj * up_proj) * 0.3989422804014327
    return (up_proj * cumulative, cumulative + up_proj * density)


def mlp_block(middle, gain_two, up_weight, down_weight, cotangent):
    normal, inverse = norm_stats(middle)
    normed = (normal * gain_two).astype(jnp.bfloat16)
    up_proj = jnp.dot(normed, up_weight, preferred_element_type=jnp.float32)
    active, slope = gelu_pair(up_proj)
    active = active.astype(jnp.bfloat16)
    output = (
        middle.astype(jnp.float32)
        + jnp.dot(active, down_weight, preferred_element_type=jnp.float32)
    ).astype(jnp.bfloat16)
    grad_down = jnp.dot(active.T, cotangent, preferred_element_type=jnp.float32)
    delta_act = jnp.dot(cotangent, down_weight.T, preferred_element_type=jnp.float32)
    delta_up = (delta_act * slope).astype(jnp.bfloat16)
    grad_up = jnp.dot(normed.T, delta_up, preferred_element_type=jnp.float32)
    delta_hidden = jnp.dot(delta_up, up_weight.T, preferred_element_type=jnp.float32)
    delta_input, grad_gain = norm_back(delta_hidden, normal, inverse, gain_two)
    delta_middle = (cotangent.astype(jnp.float32) + delta_input).astype(jnp.bfloat16)
    return (output, delta_middle, grad_gain, grad_up, grad_down)


def to_windows(layout):
    levels, lat_rows, lon_cols, features = layout.shape
    layout = layout.reshape(
        levels // WZ, WZ, lat_rows // WLAT, WLAT, lon_cols // WLON, WLON, features
    )
    layout = layout.transpose(2, 0, 4, 1, 3, 5, 6)
    return layout.reshape(
        lat_rows // WLAT, levels // WZ, lon_cols // WLON, WZ * WLAT * WLON, features
    )


def from_windows(windows, levels, lat_rows, lon_cols):
    features = windows.shape[-1]
    windows = windows.reshape(
        lat_rows // WLAT, levels // WZ, lon_cols // WLON, WZ, WLAT, WLON, features
    )
    windows = windows.transpose(1, 3, 0, 4, 2, 5, 6)
    return windows.reshape(levels, lat_rows, lon_cols, features)


def roll_grid(layout, toward):
    layout = jnp.roll(layout, toward, axis=0)
    rows_half = WLAT // 2
    cols_half = WLON // 2
    row_count = layout.shape[1]
    row_piece = layout[:, :rows_half] if toward < 0 else layout[:, row_count - rows_half :]
    row_got = passed_along(row_piece, "lat", toward)
    layout = jnp.concatenate(
        (
            (layout[:, rows_half:], row_got)
            if toward < 0
            else (row_got, layout[:, : row_count - rows_half])
        ),
        axis=1,
    )
    col_count = layout.shape[2]
    col_piece = layout[:, :, :cols_half] if toward < 0 else layout[:, :, col_count - cols_half :]
    col_got = passed_along(col_piece, "lon", toward)
    layout = jnp.concatenate(
        (
            (layout[:, :, cols_half:], col_got)
            if toward < 0
            else (col_got, layout[:, :, : col_count - cols_half])
        ),
        axis=2,
    )
    return layout


def bias_pairs(bias_table, pos_index):
    head_count, level_blocks, lat_blocks = bias_table.shape[:3]
    picked = jnp.take(bias_table, pos_index.reshape(-1), axis=3)
    picked = picked.reshape(head_count, level_blocks, lat_blocks, WT, WT).transpose(2, 1, 0, 3, 4)
    return picked[:, :, None]


def table_grad(delta_type, pos_index):
    lat_blocks, level_blocks, head_count = delta_type.shape[:3]
    flattened = delta_type.reshape(lat_blocks, level_blocks, head_count, WT * WT).transpose(
        3, 2, 1, 0
    )
    summed = jax.ops.segment_sum(flattened, pos_index.reshape(-1), num_segments=NPOS)
    return summed.transpose(1, 2, 3, 0)


def attend(windows, mask_win, bias_win, qkv_weight):
    leading = windows.shape[:-2]
    features = windows.shape[-1]
    head_size = features // HEADS
    packed = jnp.dot(
        windows.reshape(-1, features), qkv_weight, preferred_element_type=jnp.float32
    ).astype(jnp.bfloat16)
    packed = packed.reshape(leading + (WT, 3, HEADS, head_size))
    queries = packed[..., 0, :, :]
    key_heads = packed[..., 1, :, :]
    values = packed[..., 2, :, :]
    factor = head_size ** (-0.5)
    scores = (
        jnp.einsum("...phd,...rhd->...hpr", queries, key_heads, preferred_element_type=jnp.float32)
        * factor
        + bias_win
    )
    allowed = mask_win[..., None, :, None] == mask_win[..., None, None, :]
    scores = jnp.where(allowed, scores, -1e30)
    row_top = jnp.max(scores, axis=-1, keepdims=True)
    weight = jnp.exp(scores - row_top)
    attn_prob = weight / jnp.sum(weight, axis=-1, keepdims=True)
    rounded = attn_prob.astype(jnp.bfloat16)
    mixture = jnp.einsum(
        "...hpr,...rhd->...phd", rounded, values, preferred_element_type=jnp.float32
    ).astype(jnp.bfloat16)
    return (
        mixture.reshape(leading + (WT, features)),
        (queries, key_heads, values, attn_prob, rounded),
    )


def attend_back(windows, qkv_weight, stored, delta_mixture):
    queries, key_heads, values, attn_prob, rounded = stored
    leading = windows.shape[:-2]
    features = windows.shape[-1]
    head_size = features // HEADS
    factor = head_size ** (-0.5)
    delta_heads = delta_mixture.reshape(leading + (WT, HEADS, head_size))
    delta_probs = jnp.einsum(
        "...phd,...rhd->...hpr", delta_heads, values, preferred_element_type=jnp.float32
    )
    delta_values = jnp.einsum(
        "...hpr,...phd->...rhd", rounded, delta_heads, preferred_element_type=jnp.float32
    )
    delta_scores = attn_prob * (
        delta_probs - jnp.sum(delta_probs * attn_prob, axis=-1, keepdims=True)
    )
    delta_low = delta_scores.astype(jnp.bfloat16)
    delta_query = (
        jnp.einsum(
            "...hpr,...rhd->...phd", delta_low, key_heads, preferred_element_type=jnp.float32
        )
        * factor
    )
    delta_keys = (
        jnp.einsum("...hpr,...phd->...rhd", delta_low, queries, preferred_element_type=jnp.float32)
        * factor
    )
    delta_packed = (
        jnp.stack((delta_query, delta_keys, delta_values), axis=-3)
        .astype(jnp.bfloat16)
        .reshape(-1, 3 * features)
    )
    flattened = windows.reshape(-1, features)
    grad_qkv = jnp.dot(flattened.T, delta_packed, preferred_element_type=jnp.float32)
    delta_window = jnp.dot(delta_packed, qkv_weight.T, preferred_element_type=jnp.float32).astype(
        jnp.bfloat16
    )
    return (delta_window.reshape(leading + (WT, features)), grad_qkv, delta_scores)


def local(
    tokens,
    gain_one,
    gain_two,
    qkv_weight,
    proj_weight,
    up_weight,
    down_weight,
    bias_table,
    pos_index,
    mask_ids,
    cotangent,
):
    levels, lat_rows, lon_cols, features = tokens.shape
    normal_one, inverse_one = norm_stats(tokens)
    normed = (normal_one * gain_one).astype(jnp.bfloat16)
    windows = to_windows(roll_grid(normed, -1))
    mask_win = to_windows(mask_ids[..., None])[..., 0]
    bias_win = bias_pairs(bias_table, pos_index)
    mixture, stored = attend(windows, mask_win, bias_win, qkv_weight)
    flat_mix = mixture.reshape(-1, features)
    attn_win = jnp.dot(flat_mix, proj_weight, preferred_element_type=jnp.float32).astype(
        jnp.bfloat16
    )
    attention = roll_grid(
        from_windows(attn_win.reshape(mixture.shape), levels, lat_rows, lon_cols), 1
    )
    middle = (tokens.astype(jnp.float32) + attention.astype(jnp.float32)).astype(jnp.bfloat16)
    output, delta_middle, grad_gain_two, grad_up, grad_down = mlp_block(
        middle.reshape(-1, features),
        gain_two,
        up_weight,
        down_weight,
        cotangent.reshape(-1, features),
    )
    output = output.reshape(tokens.shape)
    delta_middle = delta_middle.reshape(tokens.shape)
    delta_attn = to_windows(roll_grid(delta_middle, -1))
    flat_delta = delta_attn.reshape(-1, features)
    grad_proj = jnp.dot(flat_mix.T, flat_delta, preferred_element_type=jnp.float32)
    delta_mixture = (
        jnp.dot(flat_delta, proj_weight.T, preferred_element_type=jnp.float32)
        .astype(jnp.bfloat16)
        .reshape(mixture.shape)
    )
    delta_window, grad_qkv, delta_scores = attend_back(windows, qkv_weight, stored, delta_mixture)
    local_bias = table_grad(jnp.sum(delta_scores, axis=2), pos_index)
    delta_normed = roll_grid(from_windows(delta_window, levels, lat_rows, lon_cols), 1)
    delta_input, grad_gain_one = norm_back(
        delta_normed.astype(jnp.float32), normal_one, inverse_one, gain_one
    )
    delta_tokens = (delta_middle.astype(jnp.float32) + delta_input).astype(jnp.bfloat16)
    totals = lax.psum(
        (grad_gain_one, grad_gain_two, grad_qkv, grad_proj, grad_up, grad_down), ("lat", "lon")
    )
    grad_bias = lax.psum(local_bias.astype(jnp.bfloat16), "lon").astype(jnp.float32)
    factor = 1.0 / math.sqrt(
        levels * lat_rows * lon_cols * lax.axis_size("lat") * lax.axis_size("lon")
    )
    return (
        output,
        delta_tokens,
        totals[0] * factor,
        totals[1] * factor,
        totals[2] * factor,
        totals[3] * factor,
        totals[4] * factor,
        totals[5] * factor,
        grad_bias,
    )


def solution(mesh):
    in_specs = (
        P(None, "lat", "lon", None),
        P(),
        P(),
        P(),
        P(),
        P(),
        P(),
        P(None, None, "lat", None),
        P(),
        P(None, "lat", "lon"),
        P(None, "lat", "lon", None),
    )
    out_specs = (
        P(None, "lat", "lon", None),
        P(None, "lat", "lon", None),
        P(),
        P(),
        P(),
        P(),
        P(),
        P(),
        P(None, None, "lat", None),
    )
    return jax.shard_map(local, mesh=mesh, in_specs=in_specs, out_specs=out_specs, check_vma=False)
```

profile of v0, /device:TPU:1, one launch (start us, length us, event | category | flops | bytes accessed | tf_op | source)
XLA Modules:
  0.0 416.6 jit_solution(4072287273204668960)
XLA Ops:
  7.2 1.0 convert_reduce_fusion
  8.3 1.1 fusion.31
  9.4 1.0 fusion.26
  10.6 1.1 reshape.329
  11.6 0.3 fusion.39
  11.9 1.0 compare_and_fusion
  12.9 0.7 copy.42
  13.7 1.2 collective-permute-done
  14.9 4.6 %collective-permute-start.1 = (bf16[2,6,6,192]{3,2,1,0:T(8,128)(2,1)S(1)}, bf16[2,6,6,192]{3,2,1,0:T(8,128)(2,1)S(1)}, u32[]{:S(2)}, u32[]{:S(2)}) collective-permute-start(bf16[2,6,6,192]{3,2,1,0:T(8,128)(2,1)S(1)} %get-tuple-element.50), channel_id=1, source_target_pairs={{0,7},{1,0},{2,1},{3,2},{4,3},{5,4},{6,5},{7,6},{8,15},{9,8},{10,9... | collective-permute-start | bytes 82952 | tf_op jit(solution)/shard_map/ppermute | solution.py:21
  19.7 0.5 copy.44
  20.3 38.7 %gather_fusion = f32[20736,6]{1,0:T(8,128)} fusion(f32[6,3312]{0,1:T(8,128)S(1)} %bitcast.78, s32[21504]{0:T(1024)S(1)} %pad_clamp_fusion), kind=kCustom, calls=%fused_computation | custom fusion | bytes 1078272 | tf_op jit(solution)/shard_map/jit(_take)/gather | solution.py:120
  58.9 11.7 %copy.46 = f32[6,144,144]{1,2,0:T(8,128)S(1)} copy(f32[6,144,144]{0,2,1:T(8,128)} %bitcast.79) | data formatting | bytes 995328 | tf_op jit(solution)/shard_map/jit(_take)/gather | solution.py:120
  70.7 0.2 convolution_convert_fusion
  71.0 0.2 copy.41
  71.1 0.2 copy-done.6
  71.4 0.4 fusion.4
  71.8 0.8 fusion.56
  72.6 0.3 convolution_convert_fusion.1
  73.0 0.5 copy-done.12
  73.5 0.2 convolution_convert_fusion.4
  73.8 1.4 collective-permute-start.2
  75.2 1.2 collective-permute-done.2
  76.5 0.8 reshape.352
  77.3 4.8 %collective-permute-done.3 = bf16[2,6,6,192]{3,2,1,0:T(8,128)(2,1)S(1)} collective-permute-done((bf16[2,6,6,192]{3,2,1,0:T(8,128)(2,1)S(1)}, bf16[2,6,6,192]{3,2,1,0:T(8,128)(2,1)S(1)}, u32[]{:S(2)}, u32[]{:S(2)}) %collective-permute-start.3) | collective-permute-done | bytes 27680 | tf_op jit(solution)/shard_map/ppermute | solution.py:21
  82.3 0.2 multiply_reduce_fusion.1
  82.7 0.3 multiply_convert_fusion
  83.0 1.2 fusion.5
  84.2 0.4 multiply_reduce_fusion.2
  84.6 1.2 fusion.45
  86.1 3.4 collective-permute-start.4
  89.4 1.1 fusion.59
  90.5 0.9 collective-permute-done.4
  91.5 1.2 fusion.8
  92.7 0.7 reshape.335
  93.4 0.7 copy.55
  94.1 0.8 collective-permute-done.5
  95.1 0.2 convolution_convert_fusion.3
  95.4 1.0 convolution_bitcast_fusion
  96.4 0.3 multiply_reduce_fusion
  96.8 0.2 fusion.6
  97.1 0.2 fusion.7
  97.3 0.4 copy.53
  97.8 0.6 reshape.333
  98.4 0.3 convolution_convert_fusion.2
  98.8 0.8 collective-permute-start.6
  99.6 6.1 %copy.54 = f32[20736,6]{1,0:T(8,128)} copy(f32[20736,6]{0,1:T(8,128)S(1)} %bitcast.80) | data formatting | bytes 995328 | tf_op jit(solution)/shard_map/transpose | solution.py:127
  105.8 112.8 %scatter_custom_fusion = f32[3312,6]{1,0:T(8,128)S(1)} fusion(s32[20736]{0:T(1024)} %reshape.352, f32[20736,6]{1,0:T(8,128)} %copy.54, f32[]{:T(128)} %constant.16.clone.1), kind=kCustom, calls=%fused_computation.24 | custom fusion | flops 124416 | bytes 80000 | tf_op jit(solution)/shard_map/scatter-add | solution.py:130
  218.7 0.8 copy-done.7
  219.5 1.1 fusion.57
  220.6 0.4 collective-permute-start.7
  220.9 0.9 fusion.58
  221.8 40.5 %psum.55 = bf16[6,1,1,3312]{0,3,2,1:T(8,128)(2,1)S(1)} all-reduce(bf16[6,1,1,3312]{0,3,2,1:T(8,128)(2,1)S(1)} %convert_bitcast_fusion), channel_id=1, replica_groups=mesh['lat'=4,'lon'=8] {'lon'}, use_global_device_ids=true, to_apply=%region_20.21 | all-reduce | flops 19872 | bytes 79488 | tf_op jit(solution)/shard_map/psum | solution.py:261
  262.4 1.0 copy.57
  263.4 0.3 fusion.33
  263.7 0.2 fusion.30
  263.9 0.7 copy.56
  264.6 45.9 %all-reduce = (f32[192]{0:T(256)S(1)}, f32[192]{0:T(256)S(1)}) all-reduce(f32[192]{0:T(256)S(1)} %get-tuple-element.29, f32[192]{0:T(256)S(1)} %get-tuple-element.27), channel_id=1, replica_groups=mesh['lat'=4,'lon'=8] {'lat','lon'}, use_global_device_ids=true, to_apply=%region_12.13 | all-reduce | flops 384 | bytes 3072 | tf_op jit(solution)/shard_map/psum | solution.py:258
  310.5 0.6 broadcast_multiply_fusion.9
  311.0 0.6 broadcast_multiply_fusion.8
  311.6 92.8 %all-reduce.4.cloned.1.call-done = (f32[192,576]{1,0:T(8,128)}, f32[192,192]{1,0:T(8,128)}, f32[192,768]{1,0:T(8,128)}, f32[768,192]{0,1:T(8,128)}) async-done(((f32[192,576]{1,0:T(8,128)}, f32[192,192]{1,0:T(8,128)}, f32[192,768]{1,0:T(8,128)}, f32[768,192]{0,1:T(8,128)}), (f32[192,576]{1,0:T(8,128)}, f32[192,192]{1,0:T(8,128)}, f32[192,768]{1,0:T(8,128)}, ...) | async-done | bytes 1769488 | tf_op jit(solution)/shard_map/psum | solution.py:258
  404.4 1.9 broadcast_multiply_fusion.2
  406.4 1.6 broadcast_multiply_fusion.3
  408.0 0.9 broadcast_multiply_fusion.1
  408.9 0.9 broadcast_multiply_fusion
  (96 shorter events, 2.2 us)
Async XLA Ops:
  7.2 75.5 %copy-start = (bf16[192,768]{1,0:T(8,128)(2,1)S(1)}, bf16[192,768]{1,0:T(8,128)(2,1)}, u32[]{:S(2)}) copy-start(bf16[192,768]{1,0:T(8,128)(2,1)} %param.16) | copy-start | bytes 884740
  7.2 12.5 %copy-start.16 = (f32[6,1,1,3312]{3,2,1,0:T(1,128)S(1)}, f32[6,1,1,3312]{3,2,1,0:T(1,128)}, u32[]{:S(2)}) copy-start(f32[6,1,1,3312]{3,2,1,0:T(1,128)} %param.18) | copy-start | bytes 238468
  7.2 397.2 %all-reduce.4.cloned.1.call-start = ((), (), s32[]{:S(2)}) async-start(), calls=%async_computation | async-start | bytes 3735552 | tf_op jit(solution)/shard_map/psum | solution.py:258
  10.4 4.4 %collective-permute-start = (bf16[2,3,12,192]{3,2,1,0:T(8,128)(2,1)S(1)}, bf16[2,3,12,192]{3,2,1,0:T(8,128)(2,1)S(1)}, u32[]{:S(2)}, u32[]{:S(2)}) collective-permute-start(bf16[2,3,12,192]{3,2,1,0:T(8,128)(2,1)S(1)} %get-tuple-element.52), channel_id=1, source_target_pairs={{0,24},{8,0},{16,8},{24,16},{1,25},{9,1},{17,9},{25,17},{2,26},{10... | collective-permute-start | bytes 82952 | tf_op jit(solution)/shard_map/ppermute | solution.py:21
  14.9 55.7 %collective-permute-start.1 = (bf16[2,6,6,192]{3,2,1,0:T(8,128)(2,1)S(1)}, bf16[2,6,6,192]{3,2,1,0:T(8,128)(2,1)S(1)}, u32[]{:S(2)}, u32[]{:S(2)}) collective-permute-start(bf16[2,6,6,192]{3,2,1,0:T(8,128)(2,1)S(1)} %get-tuple-element.50), channel_id=1, source_target_pairs={{0,7},{1,0},{2,1},{3,2},{4,3},{5,4},{6,5},{7,6},{8,15},{9,8},{10,9... | collective-permute-start | bytes 82952 | tf_op jit(solution)/shard_map/ppermute | solution.py:21
  58.9 11.8 %copy-start.3 = (bf16[192,576]{1,0:T(8,128)(2,1)S(1)}, bf16[192,576]{1,0:T(8,128)(2,1)}, u32[]{:S(2)}) copy-start(bf16[192,576]{1,0:T(8,128)(2,1)} %param.14) | copy-start | bytes 663556
  70.7 0.6 copy-start.6
  72.6 0.9 copy-start.12
  72.6 3.9 copy-start.2
  72.6 4.7 %copy-start.17 = (bf16[2,6,12,192]{3,0,2,1:T(2,128)(2,1)S(1)}, bf16[2,6,12,192]{3,0,2,1:T(2,128)(2,1)}, u32[]{:S(2)}) copy-start(bf16[2,6,12,192]{3,0,2,1:T(2,128)(2,1)} %param.21) | copy-start | bytes 165892
  72.9 0.8 copy-start.13
  72.9 9.2 %copy-start.1 = (bf16[2,6,12,192]{3,0,2,1:T(2,128)(2,1)S(1)}, bf16[2,6,12,192]{3,0,2,1:T(2,128)(2,1)}, u32[]{:S(2)}) copy-start(bf16[2,6,12,192]{3,0,2,1:T(2,128)(2,1)} %param.11) | copy-start | bytes 165892
  73.0 9.7 %copy-start.18 = (f32[192]{0:T(256)S(1)}, f32[192]{0:T(256)}, u32[]{:S(2)}) copy-start(f32[192]{0:T(256)} %param.13) | copy-start | bytes 2308
  73.8 2.6 collective-permute-start.2
  76.4 5.7 %collective-permute-start.3 = (bf16[2,6,6,192]{3,2,1,0:T(8,128)(2,1)S(1)}, bf16[2,6,6,192]{3,2,1,0:T(8,128)(2,1)S(1)}, u32[]{:S(2)}, u32[]{:S(2)}) collective-permute-start(bf16[2,6,6,192]{3,2,1,0:T(8,128)(2,1)S(1)} %fusion.42), channel_id=1, source_target_pairs={{0,1},{1,2},{2,3},{3,4},{4,5},{5,6},{6,7},{7,0},{8,9},{9,10},{10,1... | collective-permute-start | bytes 82952 | tf_op jit(solution)/shard_map/ppermute | solution.py:21
  86.1 5.3 %collective-permute-start.4 = (bf16[2,3,12,192]{3,2,1,0:T(8,128)(2,1)S(1)}, bf16[2,3,12,192]{3,2,1,0:T(8,128)(2,1)S(1)}, u32[]{:S(2)}, u32[]{:S(2)}) collective-permute-start(bf16[2,3,12,192]{3,2,1,0:T(8,128)(2,1)S(1)} %get-tuple-element.46), channel_id=1, source_target_pairs={{0,24},{8,0},{16,8},{24,16},{1,25},{9,1},{17,9},{25,17},{2,26},{10... | collective-permute-start | bytes 82952 | tf_op jit(solution)/shard_map/ppermute | solution.py:21
  91.4 3.6 collective-permute-start.5
  95.1 1.3 copy-start.8
  97.3 1.1 copy-start.15
  97.3 1.1 copy-start.4
  98.8 121.7 %collective-permute-start.6 = (bf16[2,3,12,192]{3,2,1,0:T(8,128)(2,1)S(1)}, bf16[2,3,12,192]{3,2,1,0:T(8,128)(2,1)S(1)}, u32[]{:S(2)}, u32[]{:S(2)}) collective-permute-start(bf16[2,3,12,192]{3,2,1,0:T(8,128)(2,1)S(1)} %get-tuple-element.41), channel_id=1, source_target_pairs={{0,8},{8,16},{16,24},{24,0},{1,9},{9,17},{17,25},{25,1},{2,10},{10... | collective-permute-start | bytes 82952 | tf_op jit(solution)/shard_map/ppermute | solution.py:21
  218.6 0.9 copy-start.7
  218.6 2.4 copy-start.9
  218.6 2.4 copy-start.14
  220.6 42.8 %collective-permute-start.7 = (bf16[2,6,6,192]{3,2,1,0:T(8,128)(2,1)S(1)}, bf16[2,6,6,192]{3,2,1,0:T(8,128)(2,1)S(1)}, u32[]{:S(2)}, u32[]{:S(2)}) collective-permute-start(bf16[2,6,6,192]{3,2,1,0:T(8,128)(2,1)S(1)} %fusion.40), channel_id=1, source_target_pairs={{0,1},{1,2},{2,3},{3,4},{4,5},{5,6},{6,7},{7,0},{8,9},{9,10},{10,1... | collective-permute-start | bytes 82952 | tf_op jit(solution)/shard_map/ppermute | solution.py:21
  262.3 1.0 copy-start.19
  262.4 1.3 copy-start.5
  404.4 3.6 copy-start.11
  404.4 4.4 %copy-start.10 = (f32[768,192]{0,1:T(8,128)S(1)}, f32[768,192]{0,1:T(8,128)}, u32[]{:S(2)}) copy-start(f32[768,192]{0,1:T(8,128)} %get-tuple-element.38) | copy-start | bytes 1769476
Sparse Core Ops, SparseCore 0:
  263.5 140.8 all-reduce.3
where the time goes:
time: 418 us; the launch traced here: 417 us
  other arithmetic  126 us (30%)
  waiting for transfers between devices  102 us (24%)
  blocking collectives  86.4 us (21%)
  local copies, waits for them, and re-layouts  66.3 us (16%)
  between operations  14.8 us (4%)
  starting transfers between devices  10.8 us (3%)
  matrix products  10.7 us (3%)
    scatter-add x1, other arithmetic, table_grad(): jax.ops.segment_sum(flattened, pos_index.reshape(-1), num_segments=NPOS)  113 us
    psum x1, waiting for transfers between devices, local(): lax.psum((grad_gain_one, grad_gain_two, grad_qkv, grad_proj, grad_up, gra...  92.8 us
    gather x2, local copies, waits for them, and re-layouts, bias_pairs(): picked = jnp.take(bias_table, pos_index.reshape(-1), axis=3)  50.3 us
    psum x1, blocking collectives, local(): lax.psum((grad_gain_one, grad_gain_two, grad_qkv, grad_proj, grad_up, gra...  45.9 us
    psum x1, blocking collectives, local(): lax.psum(local_bias.astype(jnp.bfloat16), 'lon').astype(jnp.float32)  40.5 us
    ppermute x8, starting transfers between devices, passed_along(): return lax.ppermute(x, axis, [(i, (i + by) % peers) for i in range(peers)])  10.8 us
    ppermute x8, waiting for transfers between devices, passed_along(): return lax.ppermute(x, axis, [(i, (i + by) % peers) for i in range(peers)])  8.87 us
  transfers between devices with their start and end apart: 9, of which 6 were waited for; matrix products, arithmetic and copies ran while one was open for 44% of the time, Pallas kernels for 0%

commit v1 on v0

v1 whole, which is shorter than its diff:
```python
import functools
import math

import jax
import jax.numpy as jnp
import numpy as np
from jax import lax
from jax.experimental import pallas as pl
from jax.experimental.pallas import tpu as pltpu
from jax.sharding import PartitionSpec as P

HEADS = 6
WZ = 2
WLAT = 6
WLON = 12
WT = 144
NPOS = 3312
C = 192
HID = 768
HD = 32
SLOT = 48
NT = 4 * SLOT
LANES = 128
HI = 32
HI_USED = -(-NPOS // LANES)
EPS = 1e-05
F32 = jnp.float32
BF16 = jnp.bfloat16
MESH = pl.DeviceIdType.MESH


def orders():
    grid = np.zeros((NT, WT), np.float32)
    window = np.zeros((256, WT), np.float32)
    for rh in range(2):
        for ch in range(2):
            for z in range(2):
                for r in range(3):
                    for c in range(6):
                        row = (rh * 2 + ch) * SLOT + z * 18 + r * 6 + c
                        grid[row, z * 72 + (3 * rh + r) * 12 + 6 * ch + c] = 1
                        window[row, (1 - z) * 72 + (3 * (1 - rh) + r) * 12 + 6 * (1 - ch) + c] = 1
    return grid, window


def mm(a, b):
    return lax.dot_general(a, b, (((1,), (0,)), ((), ())), preferred_element_type=F32)


def mm_nt(a, b):
    return lax.dot_general(a, b, (((1,), (1,)), ((), ())), preferred_element_type=F32)


def mm_tn(a, b):
    return lax.dot_general(a, b, (((0,), (0,)), ((), ())), preferred_element_type=F32)


def norm_stats(widened):
    center = widened - jnp.mean(widened, axis=-1, keepdims=True)
    spread = jnp.mean(center * center, axis=-1, keepdims=True)
    inverse = lax.rsqrt(spread + EPS)
    return center * inverse, inverse


def norm_back(delta_hidden, normal, inverse, gain):
    grad_gain = jnp.sum(delta_hidden * normal, axis=0, keepdims=True)
    delta_normal = delta_hidden * gain
    delta_input = inverse * (
        delta_normal
        - jnp.mean(delta_normal, axis=-1, keepdims=True)
        - normal * jnp.mean(delta_normal * normal, axis=-1, keepdims=True)
    )
    return delta_input, grad_gain


class Exchange:
    def __init__(self, place, axis, send_sem, recv_sem):
        self.lat, self.lon, self.n_lat, self.n_lon = place
        self.axis = axis
        self.n = self.n_lat if axis == 0 else self.n_lon
        self.me = self.lat if axis == 0 else self.lon
        self.send_sem, self.recv_sem = send_sem, recv_sem
        self.copies = []

    def peer(self, d):
        to = lax.rem(self.me + d, self.n)
        return to, ((to, self.lon) if self.axis == 0 else (self.lat, to))

    def start(self, d, src, dst, device):
        copy = pltpu.make_async_remote_copy(
            src_ref=src,
            dst_ref=dst,
            send_sem=self.send_sem.at[d - 1],
            recv_sem=self.recv_sem.at[d - 1],
            device_id=device,
            device_id_type=MESH,
        )
        copy.start()
        self.copies.append(copy)

    def scatter(self, src, got, rows):
        self.src, self.got, self.rows = src, got, rows
        for d in range(1, self.n):
            to, device = self.peer(d)
            piece = pl.ds(pl.multiple_of(to * rows, 16), rows)
            self.start(d, src.at[piece], got.at[pl.ds((d - 1) * rows, rows)], device)

    def gather(self, whole, rows, start):
        piece = pl.ds(start, rows)
        for d in range(1, self.n):
            _, device = self.peer(d)
            self.start(d, whole.at[piece], whole.at[piece], device)

    def wait(self):
        for copy in self.copies:
            copy.wait()

    def total(self):
        self.wait()
        rows = self.rows
        own = pl.ds(pl.multiple_of(self.me * rows, 16), rows)
        out = self.src[own, :].astype(F32)
        for d in range(1, self.n):
            out = out + self.got[pl.ds((d - 1) * rows, rows), :].astype(F32)
        return out


def kernel(
    n_lat,
    n_lon,
    factor,
    rp1,
    rp2,
    rpb,
    tokens_ref,
    cot_ref,
    gain1_ref,
    gain2_ref,
    wqkv_ref,
    wproj_ref,
    wup_ref,
    wdown_ref,
    table_ref,
    pos_ref,
    mask_ref,
    grid_ref,
    win_ref,
    out_ref,
    dtok_ref,
    ggain_ref,
    gqkv_ref,
    gproj_ref,
    gup_ref,
    gdown_ref,
    gbias_ref,
    xs,
    xr,
    hi_ref,
    lo_ref,
    bias_ref,
    prob_ref,
    ds_ref,
    mix_ref,
    dpk_ref,
    pack_ref,
    gains_ref,
    buf1,
    got1,
    mid1,
    gom1,
    all1,
    buf2,
    got2,
    mid2,
    gom2,
    all2,
    bufb,
    gotb,
    allb,
    x_send,
    x_recv,
    lat_send,
    lat_recv,
    lon_send,
    lon_recv,
):
    lat, lon = lax.axis_index("lat"), lax.axis_index("lon")
    place = (lat, lon, n_lat, n_lon)
    next_lat, next_lon = lax.rem(lat + 1, n_lat), lax.rem(lon + 1, n_lon)
    prev_lat, prev_lon = lax.rem(lat + n_lat - 1, n_lat), lax.rem(lon + n_lon - 1, n_lon)
    befores = ((prev_lat, prev_lon), (prev_lat, lon), (lat, prev_lon))
    afters = ((next_lat, next_lon), (next_lat, lon), (lat, next_lon))

    barrier = pltpu.get_barrier_semaphore()
    peers = [(lax.rem(lat + d, n_lat), lon) for d in range(1, n_lat)]
    peers += [(lat, lax.rem(lon + d, n_lon)) for d in range(1, n_lon)]
    peers += [befores[0], afters[0]]
    for peer in peers:
        pl.semaphore_signal(barrier, inc=1, device_id=peer, device_id_type=MESH)

    def send_slots(e, devices):
        copies = []
        for s in range(3):
            piece = pl.ds(s * SLOT, SLOT)
            copy = pltpu.make_async_remote_copy(
                src_ref=xs.at[e, piece],
                dst_ref=xr.at[e, piece],
                send_sem=x_send.at[e, s],
                recv_sem=x_recv.at[e, s],
                device_id=devices[s],
                device_id_type=MESH,
            )
            copy.start()
            copies.append(copy)
        xr[e, 3 * SLOT :, :] = xs[e, 3 * SLOT :, :]
        return copies

    def finish(copies):
        for copy in copies:
            copy.wait()

    grid = grid_ref[...]
    tokens = mm(grid, tokens_ref[...])
    normal_one, inverse_one = norm_stats(tokens)
    gain_one = gain1_ref[...]
    xs[0] = (normal_one * gain_one).astype(BF16)
    pl.semaphore_wait(barrier, len(peers))
    copies = send_slots(0, befores)

    win = win_ref[...]
    win_rows = win[:NT]
    pos = pos_ref[...]
    hi = (pos >> 7).astype(F32).astype(BF16)
    lo = (pos & 127).astype(F32).astype(BF16)
    hi_ref[...] = mm_nt(mm(win_rows, hi).astype(BF16), win).astype(jnp.int32)
    lo_ref[...] = mm_nt(mm(win_rows, lo).astype(BF16), win).astype(jnp.int32)
    mask = jnp.broadcast_to((mask_ref[...] + 1).astype(F32), (8, WT)).astype(BF16)
    mask_row = mm_nt(mask, win)[0:1, :]
    mask_col = mm_nt(win_rows, mask)[:, 0:1]
    prob_ref[0] = jnp.where(mask_col == mask_row, 0.0, -1e30)

    step = 16

    def pick(block, carry):
        rows = pl.ds(pl.multiple_of(block * step, step), step)
        for half in range(2):
            cols = pl.ds(half * LANES, LANES)
            hi_here, lo_here = hi_ref[rows, cols], lo_ref[rows, cols]
            drop = prob_ref[0, rows, cols]
            acc = [drop] * HEADS
            for k in range(HI_USED):
                here = hi_here == k
                for h in range(HEADS):
                    row = jnp.broadcast_to(table_ref[pl.ds(h * HI + k, 1), :], (step, LANES))
                    got = jnp.take_along_axis(row, lo_here, axis=1, mode="promise_in_bounds")
                    acc[h] = jnp.where(here, got + drop, acc[h])
            for h in range(HEADS):
                bias_ref[h, rows, cols] = acc[h]
        return carry

    lax.fori_loop(0, NT // step, pick, 0)

    finish(copies)
    windows = xr[0]
    packed = mm(windows, wqkv_ref[...]).astype(BF16)
    scale = HD**-0.5

    def head(h, part):
        return packed[:, part * C + h * HD : part * C + (h + 1) * HD]

    for h in range(HEADS):
        scores = mm_nt(head(h, 0), head(h, 1)) * scale + bias_ref[h, :, :NT]
        weight = jnp.exp(scores - jnp.max(scores, axis=-1, keepdims=True))
        prob = weight / jnp.sum(weight, axis=-1, keepdims=True)
        prob_ref[h, :, :NT] = prob
        mix_ref[:, h * HD : (h + 1) * HD] = mm(prob.astype(BF16), head(h, 2))
    mixture = mix_ref[...].astype(BF16)
    xs[1] = mm(mixture, wproj_ref[...]).astype(BF16)
    copies = send_slots(1, afters)

    cot = mm(grid, cot_ref[...]).astype(BF16)
    delta_act = mm_nt(cot, wdown_ref[...])
    buf1[2304:, :] = jnp.zeros((buf1.shape[0] - 2304, LANES), BF16)
    buf2[1152:, :] = jnp.zeros((buf2.shape[0] - 1152, LANES), BF16)
    bufb[...] = jnp.zeros(bufb.shape, BF16)
    ds_ref[...] = jnp.zeros(ds_ref.shape, F32)
    gains_ref[...] = jnp.zeros(gains_ref.shape, F32)
    finish(copies)

    middle = (tokens + xr[1].astype(F32)).astype(BF16).astype(F32)
    normal_two, inverse_two = norm_stats(middle)
    gain_two = gain2_ref[...]
    normed_two = (normal_two * gain_two).astype(BF16)
    up = mm(normed_two, wup_ref[...])
    cumulative = 0.5 * (1.0 + lax.erf(up * 0.7071067811865476))
    density = jnp.exp(-0.5 * up * up) * 0.3989422804014327
    active = (up * cumulative).astype(BF16)
    delta_up = (delta_act * (cumulative + up * density)).astype(BF16)
    delta_hidden = mm_nt(delta_up, wup_ref[...])
    delta_input, grad_gain_two = norm_back(delta_hidden, normal_two, inverse_two, gain_two)
    delta_middle = (cot.astype(F32) + delta_input).astype(BF16)
    xs[2] = delta_middle
    copies = send_slots(2, befores)

    grad_up = mm_tn(normed_two, delta_up).astype(BF16)
    for j in range(6):
        buf1[j * C : (j + 1) * C, :] = grad_up[:, j * LANES : (j + 1) * LANES]
    grad_down = mm_tn(active, cot)
    buf1[1152:1920, :] = grad_down[:, :LANES].astype(BF16)
    pack_ref[:HID // 2, :64] = grad_down[: HID // 2, LANES:]
    pack_ref[:HID // 2, 64:128] = grad_down[HID // 2 :, LANES:]
    buf1[1920:2304, :] = pack_ref[: HID // 2, :LANES].astype(BF16)

    def exchange(axis, k):
        if axis == 0:
            return Exchange(place, 0, lat_send.at[k], lat_recv.at[k])
        return Exchange(place, 1, lon_send.at[k], lon_recv.at[k])

    rq1, rq2 = rp1 * n_lon, rp2 * n_lon
    scatter_lat1 = exchange(0, 0)
    scatter_lat1.scatter(buf1, got1, rq1)
    output = middle + mm(active, wdown_ref[...])
    out_ref[...] = mm_tn(grid, output.astype(BF16)).astype(BF16)
    finish(copies)

    delta_attn = xr[2]
    delta_mix = mm_nt(delta_attn, wproj_ref[...]).astype(BF16)
    pack_ref[:C, 3 * C :] = mm_tn(mixture, delta_attn)
    for h in range(HEADS):
        cols = slice(h * HD, (h + 1) * HD)
        delta_head = delta_mix[:, cols]
        prob = prob_ref[h, :, :NT]
        delta_prob = mm_nt(delta_head, head(h, 2))
        scored = prob * (delta_prob - jnp.sum(delta_prob * prob, axis=-1, keepdims=True))
        ds_ref[h, :, :NT] = scored
        low = scored.astype(BF16)
        dpk_ref[:, h * HD : (h + 1) * HD] = mm(low, head(h, 1)) * scale
        dpk_ref[:, C + h * HD : C + (h + 1) * HD] = mm_tn(low, head(h, 0)) * scale
        dpk_ref[:, 2 * C + h * HD : 2 * C + (h + 1) * HD] = mm_tn(prob.astype(BF16), delta_head)
    delta_packed = dpk_ref[...].astype(BF16)
    xs[3] = mm_nt(delta_packed, wqkv_ref[...]).astype(BF16)
    copies = send_slots(3, afters)

    mid1[...] = scatter_lat1.total().astype(BF16)
    scatter_lon1 = exchange(1, 0)
    scatter_lon1.scatter(mid1, gom1, rp1)
    pack_ref[:C, : 3 * C] = mm_tn(windows, delta_packed)
    for j in range(6):
        buf2[j * C : (j + 1) * C, :] = pack_ref[:C, j * LANES : (j + 1) * LANES].astype(BF16)
    finish(copies)

    delta_normed = xr[3].astype(F32)
    delta_input, grad_gain_one = norm_back(delta_normed, normal_one, inverse_one, gain_one)
    gains_ref[0:1, :C] = grad_gain_one
    gains_ref[1:2, :C] = grad_gain_two
    buf2[1152:1168, :] = gains_ref[:, :LANES].astype(BF16)
    buf2[1168:1184, :] = gains_ref[:, LANES:].astype(BF16)
    scatter_lat2 = exchange(0, 1)
    scatter_lat2.scatter(buf2, got2, rq2)
    delta_tokens = (delta_middle.astype(F32) + delta_input).astype(BF16)
    dtok_ref[...] = mm_tn(grid, delta_tokens).astype(BF16)

    def own_rows(rows):
        return pl.multiple_of((lat * n_lon + lon) * rows, 16)

    start1 = own_rows(rp1)
    all1[pl.ds(start1, rp1), :] = (scatter_lon1.total() * factor).astype(BF16)
    gather_lon1 = exchange(1, 1)
    gather_lon1.gather(all1, rp1, start1)

    iota_hi = lax.broadcasted_iota(jnp.int32, (HI, 256), 0)
    iota_lo = lax.broadcasted_iota(jnp.int32, (LANES, 256), 0)

    def collect(block, acc):
        slot = block // 5
        rows = pl.ds(pl.multiple_of(slot * SLOT + (block - slot * 5) * 8, 8), 8)
        hi_rows, lo_rows = hi_ref[rows, :], lo_ref[rows, :]
        ds_rows = [ds_ref[h, rows, :] for h in range(HEADS)]
        left, right = [], []
        for i in range(8):
            here = iota_hi == hi_rows[i : i + 1, :]
            left.append(
                jnp.concatenate(
                    [jnp.where(here, rows_h[i : i + 1, :], 0.0).astype(BF16) for rows_h in ds_rows],
                    axis=0,
                )
            )
            right.append(
                jnp.where(iota_lo == lo_rows[i : i + 1, :], 1.0, 0.0).astype(BF16)
            )
        return acc + mm_nt(jnp.concatenate(left, axis=1), jnp.concatenate(right, axis=1))

    bias_sum = lax.fori_loop(0, 20, collect, jnp.zeros((HEADS * HI, LANES), F32))
    bufb[: HEADS * HI, :] = bias_sum.astype(BF16)
    scatter_b = exchange(1, 2)
    scatter_b.scatter(bufb, gotb, rpb)

    mid2[...] = scatter_lat2.total().astype(BF16)
    scatter_lon2 = exchange(1, 3)
    scatter_lon2.scatter(mid2, gom2, rp2)

    gather_lon1.wait()
    gather_lat1 = exchange(0, 2)
    gather_lat1.gather(all1, rq1, pl.multiple_of(lat * rq1, 16))

    startb = pl.multiple_of(lon * rpb, 16)
    allb[pl.ds(startb, rpb), :] = scatter_b.total().astype(BF16)
    gather_b = exchange(1, 4)
    gather_b.gather(allb, rpb, startb)

    start2 = own_rows(rp2)
    all2[pl.ds(start2, rp2), :] = (scatter_lon2.total() * factor).astype(BF16)
    gather_lon2 = exchange(1, 5)
    gather_lon2.gather(all2, rp2, start2)
    gather_lon2.wait()
    gather_lat2 = exchange(0, 3)
    gather_lat2.gather(all2, rq2, pl.multiple_of(lat * rq2, 16))

    gather_b.wait()
    gbias_ref[...] = allb[: HEADS * HI, :].astype(F32)
    gather_lat1.wait()
    for j in range(6):
        gup_ref[:, j * LANES : (j + 1) * LANES] = all1[j * C : (j + 1) * C, :].astype(F32)
    gdown_ref[:, :LANES] = all1[1152:1920, :].astype(F32)
    tail = all1[1920:2304, :].astype(F32)
    gdown_ref[: HID // 2, LANES:] = tail[:, :64]
    gdown_ref[HID // 2 :, LANES:] = tail[:, 64:]
    gather_lat2.wait()
    for j in range(6):
        pack_ref[:C, j * LANES : (j + 1) * LANES] = all2[j * C : (j + 1) * C, :].astype(F32)
    gqkv_ref[...] = pack_ref[:C, : 3 * C]
    gproj_ref[...] = pack_ref[:C, 3 * C :]
    ggain_ref[:, :LANES] = all2[1152:1168, :].astype(F32)
    ggain_ref[:, LANES:] = all2[1168:1184, :].astype(F32)


def up_to(value, unit):
    return -(-value // unit) * unit


def local(
    n_lat,
    n_lon,
    tokens,
    gain_one,
    gain_two,
    qkv_weight,
    proj_weight,
    up_weight,
    down_weight,
    bias_table,
    pos_index,
    mask_ids,
    cotangent,
):
    n = n_lat * n_lon
    factor = 1.0 / math.sqrt(WT * n)
    rp1 = up_to(-(-2304 // n), 16)
    rp2 = up_to(-(-1184 // n), 16)
    rpb = up_to(-(-HEADS * HI // n_lon), 16)
    grid, window = orders()
    table = jnp.pad(bias_table.reshape(HEADS, NPOS), ((0, 0), (0, HI * LANES - NPOS)))
    args = (
        tokens.reshape(WT, C),
        cotangent.reshape(WT, C),
        gain_one.reshape(1, C),
        gain_two.reshape(1, C),
        qkv_weight,
        proj_weight,
        up_weight,
        down_weight,
        table.reshape(HEADS * HI, LANES),
        pos_index,
        mask_ids.reshape(1, WT),
        jnp.asarray(grid, BF16),
        jnp.asarray(window, BF16),
    )
    shape = jax.ShapeDtypeStruct
    outs = (
        shape((WT, C), BF16),
        shape((WT, C), BF16),
        shape((16, 256), F32),
        shape((C, 3 * C), F32),
        shape((C, C), F32),
        shape((C, HID), F32),
        shape((HID, C), F32),
        shape((HEADS * HI, LANES), F32),
    )

    def rows(count):
        return pltpu.VMEM((count, LANES), BF16)

    dma = pltpu.SemaphoreType.DMA
    scratch = [
        pltpu.VMEM((4, NT, C), BF16),
        pltpu.VMEM((4, NT, C), BF16),
        pltpu.VMEM((NT, 256), jnp.int32),
        pltpu.VMEM((NT, 256), jnp.int32),
        pltpu.VMEM((HEADS, NT, 256), F32),
        pltpu.VMEM((HEADS, NT, 256), F32),
        pltpu.VMEM((HEADS, NT, 256), F32),
        pltpu.VMEM((NT, C), F32),
        pltpu.VMEM((NT, 3 * C), F32),
        pltpu.VMEM((HID // 2, HID), F32),
        pltpu.VMEM((16, 256), F32),
    ]
    for rp in (rp1, rp2):
        scratch += [
            rows(rp * n),
            rows(rp * n_lon * (n_lat - 1)),
            rows(rp * n_lon),
            rows(rp * (n_lon - 1)),
            rows(rp * n),
        ]
    scratch += [rows(rpb * n_lon), rows(rpb * (n_lon - 1)), rows(rpb * n_lon)]
    scratch += [
        dma((4, 3)),
        dma((4, 3)),
        dma((4, n_lat - 1)),
        dma((4, n_lat - 1)),
        dma((6, n_lon - 1)),
        dma((6, n_lon - 1)),
    ]
    vmem = pl.BlockSpec(memory_space=pltpu.VMEM)
    out, dtok, ggain, gqkv, gproj, gup, gdown, gbias = pl.pallas_call(
        functools.partial(kernel, n_lat, n_lon, factor, rp1, rp2, rpb),
        out_shape=outs,
        in_specs=[vmem] * len(args),
        out_specs=[vmem] * len(outs),
        scratch_shapes=scratch,
        compiler_params=pltpu.CompilerParams(
            collective_id=0, has_side_effects=True, vmem_limit_bytes=48 * 1024 * 1024
        ),
    )(*args)
    return (
        out.reshape(tokens.shape),
        dtok.reshape(tokens.shape),
        ggain[0, :C],
        ggain[1, :C],
        gqkv,
        gproj,
        gup,
        gdown,
        gbias.reshape(HEADS, HI * LANES)[:, :NPOS].reshape(bias_table.shape),
    )


def solution(mesh):
    grid = P(None, "lat", "lon", None)
    table = P(None, None, "lat", None)
    in_specs = (grid, P(), P(), P(), P(), P(), P(), table, P(), P(None, "lat", "lon"), grid)
    out_specs = (grid, grid, P(), P(), P(), P(), P(), P(), table)
    body = functools.partial(local, mesh.shape["lat"], mesh.shape["lon"])
    return jax.shard_map(
        body, mesh=mesh, in_specs=in_specs, out_specs=out_specs, check_vma=False
    )
```

time: 418 us -> 81.4 us (0.19)
  other arithmetic: 126 us -> 0 us
  waiting for transfers between devices: 102 us -> 0 us
  blocking collectives: 86.4 us -> 0 us
  Pallas kernels: 0 us -> 63.6 us
  local copies, waits for them, and re-layouts: 66.3 us -> 16.5 us
  between operations: 14.8 us -> 0.8 us
  starting transfers between devices: 10.8 us -> 0 us
  matrix products: 10.7 us -> 0 us
    scatter-add x1 -> x0, other arithmetic: 113 us -> none  [table_grad(): jax.ops.segment_sum(flattened, pos_index.reshape(-1), num_segments=NPOS)]
    psum x1 -> x0, waiting for transfers between devices: 92.8 us -> none  [local(): lax.psum((grad_gain_one, grad_gain_two, grad_qkv, grad_proj, grad_up, gra...]
    psum x2 -> x0, blocking collectives: 86.4 us -> none  [the longest x1 45.9 us: local(): lax.psum((grad_gain_one, grad_gain_two, grad_qkv, grad_proj, grad_up, gra...]
    pallas_call x0 -> x1, Pallas kernels: none -> 63.6 us  [local(): pl.pallas_call(functools.partial(kernel, n_lat, n_lon, factor, rp1, rp2,...]
    gather x2 -> x0, local copies, waits for them, and re-layouts: 50.3 us -> none  [bias_pairs(): picked = jnp.take(bias_table, pos_index.reshape(-1), axis=3)]
    ppermute x8 -> x0, starting transfers between devices: 10.8 us -> none  [passed_along(): return lax.ppermute(x, axis, [(i, (i + by) % peers) for i in range(peers)])]
    dot_general x18 -> x0, matrix products: 10.7 us -> none  [the longest x1 1.23 us: mlp_block(): jnp.dot(cotangent, down_weight.T, preferred_element_type=jnp.float32)]
    ppermute x8 -> x0, waiting for transfers between devices: 8.87 us -> none  [passed_along(): return lax.ppermute(x, axis, [(i, (i + by) % peers) for i in range(peers)])]
  transfers between devices with their start and end apart: 9 -> 0, of which waited for: 6 -> 0; matrix products, arithmetic and copies ran while one was open for 44% -> 0% of each run, Pallas kernels for 0% -> 0%
where the time goes in v1:
time: 81.4 us; the launch traced here: 80.9 us
  Pallas kernels  63.6 us (78%)
  local copies, waits for them, and re-layouts  16.5 us (20%)
    pallas_call x1, Pallas kernels, local(): pl.pallas_call(functools.partial(kernel, n_lat, n_lon, factor, rp1, rp2,...  63.6 us
    unnamed x43, local copies, waits for them, and re-layouts  14 us

profile of v1, /device:TPU:1, one launch (start us, length us, event | category | flops | bytes accessed | tf_op | source)
XLA Modules:
  0.0 80.9 jit_solution(5449503299350313097)
XLA Ops:
  0.6 0.7 copy.31
  1.3 0.1 reshape.57.mask_ref
  1.4 0.9 %copy.29 = bf16[2,6,12,192]{3,2,1,0:T(8,128)(2,1)S(1)} copy(bf16[2,6,12,192]{3,0,2,1:T(2,128)(2,1)} %param.13) | data formatting | bytes 110592 | tf_op args[0]
  2.3 0.0 copy-start.15
  2.4 0.8 %copy-done.15 = bf16[2,6,12,192]{3,0,2,1:T(2,128)(2,1)S(1)} copy-done((bf16[2,6,12,192]{3,0,2,1:T(2,128)(2,1)S(1)}, bf16[2,6,12,192]{3,0,2,1:T(2,128)(2,1)}, u32[]{:S(2)}) %copy-start.15) | copy-done | bytes 55320
  3.2 0.0 copy-start.14
  3.3 0.8 %copy-done.14 = f32[6,1,1,3312]{3,2,1,0:T(1,128)S(1)} copy-done((f32[6,1,1,3312]{3,2,1,0:T(1,128)S(1)}, f32[6,1,1,3312]{3,2,1,0:T(1,128)}, u32[]{:S(2)}) %copy-start.14) | copy-done | bytes 79512
  4.1 0.0 copy-start.13
  4.2 0.0 copy-start.3
  4.2 0.0 copy-start.11
  4.2 0.0 copy-start.12
  4.2 0.1 reshape.56.table_ref
  4.3 0.8 %copy-done.13 = bf16[768,192]{0,1:T(8,128)(2,1)S(1)} copy-done((bf16[768,192]{0,1:T(8,128)(2,1)S(1)}, bf16[768,192]{0,1:T(8,128)(2,1)}, u32[]{:S(2)}) %copy-start.13) | copy-done | bytes 294936
  5.1 0.0 copy-start
  5.1 0.0 copy-start.1
  5.1 0.0 copy-start.2
  5.1 0.2 copy.32.wdown_ref
  5.3 0.0 copy-done.3
  5.3 0.0 copy-done.11
  5.3 0.0 copy-done.12
  5.3 0.8 copy-done
  6.1 0.1 copy-done.1
  6.1 0.1 copy-done.2
  6.2 0.0 copy-start.4
  6.2 0.9 %copy-done.4 = bf16[192,192]{1,0:T(8,128)(2,1)S(1)} copy-done((bf16[192,192]{1,0:T(8,128)(2,1)S(1)}, bf16[192,192]{1,0:T(8,128)(2,1)}, u32[]{:S(2)}) %copy-start.4) | copy-done | bytes 73752
  7.1 0.0 copy-start.5
  7.1 0.9 %copy-done.5 = bf16[192,144]{1,0:T(8,128)(2,1)S(1)} copy-done((bf16[192,144]{1,0:T(8,128)(2,1)S(1)}, bf16[192,144]{1,0:T(8,128)(2,1)}, u32[]{:S(2)}) %copy-start.5) | copy-done | bytes 55320
  8.0 63.6 %shard_map.196 = (bf16[144,192]{1,0:T(8,128)(2,1)S(1)}, bf16[144,192]{1,0:T(8,128)(2,1)S(1)}, f32[16,256]{1,0:T(8,128)S(1)}, f32[192,576]{1,0:T(8,128)S(1)}, f32...) custom-call(bf16[144,192]{1,0:T(8,128)(2,1)S(1)} %reshape.51.tokens_ref, ...), custom_call_target="tpu_custom_call" | custom-call | tf_op jit(solution)/shard_map/pallas_call | solution.py:525
  71.6 0.0 copy-start.6
  71.6 0.6 copy-done.6
  72.3 0.0 copy-start.8
  72.3 0.6 copy-done.8
  72.9 0.0 copy-start.10
  72.9 0.6 copy-done.10
  73.5 0.6 fusion
  74.1 0.9 %reshape.58 = bf16[2,6,12,192]{3,2,1,0:T(8,128)(2,1)S(1)} reshape(bf16[144,192]{1,0:T(8,128)(2,1)} %copy-done.10) | data formatting | bytes 110592 | tf_op jit(solution)/shard_map/reshape | solution.py:536
  75.0 0.0 copy-start.9
  75.0 0.7 copy.33
  75.7 0.2 copy-done.9
  75.9 0.0 copy-start.7
  76.0 0.7 copy.34
  76.7 0.2 copy-done.7
  76.9 0.7 reshape.61
  77.6 1.1 %copy.35 = f32[768,192]{0,1:T(8,128)} copy(f32[768,192]{1,0:T(8,128)S(1)} %get-tuple-element.41) | data formatting | bytes 1179648
  78.6 0.8 copy.42
  79.4 0.7 copy.43
  80.1 0.8 %copy.44 = f32[192,768]{1,0:T(8,128)} copy(f32[192,768]{1,0:T(8,128)S(1)} %get-tuple-element.60) | data formatting | bytes 1179648
  (8 shorter events, 0.2 us)
Async XLA Ops:
  2.3 0.9 %copy-start.15 = (bf16[2,6,12,192]{3,0,2,1:T(2,128)(2,1)S(1)}, bf16[2,6,12,192]{3,0,2,1:T(2,128)(2,1)}, u32[]{:S(2)}) copy-start(bf16[2,6,12,192]{3,0,2,1:T(2,128)(2,1)} %param.23) | copy-start | bytes 165892
  3.2 0.9 %copy-start.14 = (f32[6,1,1,3312]{3,2,1,0:T(1,128)S(1)}, f32[6,1,1,3312]{3,2,1,0:T(1,128)}, u32[]{:S(2)}) copy-start(f32[6,1,1,3312]{3,2,1,0:T(1,128)} %param.20) | copy-start | bytes 238468
  4.1 1.0 %copy-start.13 = (bf16[768,192]{0,1:T(8,128)(2,1)S(1)}, bf16[768,192]{0,1:T(8,128)(2,1)}, u32[]{:S(2)}) copy-start(bf16[768,192]{0,1:T(8,128)(2,1)} %param.19) | copy-start | bytes 884740
  4.2 1.1 %copy-start.3 = (bf16[256,144]{1,0:T(8,128)(2,1)S(1)}, bf16[256,144]{1,0:T(8,128)(2,1)}, u32[]{:S(2)}) copy-start(bf16[256,144]{1,0:T(8,128)(2,1)} %constant.8.clone.win_ref) | copy-start | bytes 221188
  4.2 1.1 %copy-start.11 = (f32[192]{0:T(256)S(1)}, f32[192]{0:T(256)}, u32[]{:S(2)}) copy-start(f32[192]{0:T(256)} %param.14) | copy-start | bytes 2308
  4.2 1.1 %copy-start.12 = (f32[192]{0:T(256)S(1)}, f32[192]{0:T(256)}, u32[]{:S(2)}) copy-start(f32[192]{0:T(256)} %param.15) | copy-start | bytes 2308
  5.1 1.0 %copy-start = (bf16[192,768]{1,0:T(8,128)(2,1)S(1)}, bf16[192,768]{1,0:T(8,128)(2,1)}, u32[]{:S(2)}) copy-start(bf16[192,768]{1,0:T(8,128)(2,1)} %wup_ref.1) | copy-start | bytes 884740
  5.1 1.0 %copy-start.1 = (bf16[192,576]{1,0:T(8,128)(2,1)S(1)}, bf16[192,576]{1,0:T(8,128)(2,1)}, u32[]{:S(2)}) copy-start(bf16[192,576]{1,0:T(8,128)(2,1)} %wqkv_ref.1) | copy-start | bytes 663556
  5.1 1.1 %copy-start.2 = (s32[144,144]{1,0:T(8,128)S(1)}, s32[144,144]{1,0:T(8,128)}, u32[]{:S(2)}) copy-start(s32[144,144]{1,0:T(8,128)} %pos_ref.1) | copy-start | bytes 248836
  6.2 0.9 %copy-start.4 = (bf16[192,192]{1,0:T(8,128)(2,1)S(1)}, bf16[192,192]{1,0:T(8,128)(2,1)}, u32[]{:S(2)}) copy-start(bf16[192,192]{1,0:T(8,128)(2,1)} %wproj_ref.1) | copy-start | bytes 221188
  7.1 0.9 %copy-start.5 = (bf16[192,144]{1,0:T(8,128)(2,1)S(1)}, bf16[192,144]{1,0:T(8,128)(2,1)}, u32[]{:S(2)}) copy-start(bf16[192,144]{1,0:T(8,128)(2,1)} %constant.7.clone.grid_ref) | copy-start | bytes 165892
  71.6 0.6 copy-start.6
  72.3 0.6 copy-start.8
  72.9 0.6 copy-start.10
  75.0 0.9 %copy-start.9 = (bf16[144,192]{1,0:T(8,128)(2,1)S(1)}, bf16[144,192]{1,0:T(8,128)(2,1)}, u32[]{:S(2)}) copy-start(bf16[144,192]{1,0:T(8,128)(2,1)} %copy-done.8) | copy-start | bytes 165892
  75.9 0.9 %copy-start.7 = (f32[192,128]{1,0:T(8,128)S(1)}, f32[192,128]{1,0:T(8,128)}, u32[]{:S(2)}) copy-start(f32[192,128]{1,0:T(8,128)} %copy-done.6) | copy-start | bytes 294916

commit v2 on v1

--- a/solution.py
+++ b/solution.py
@@ -136,23 +136,29 @@
     cot_ref,
     gain1_ref,
     gain2_ref,
+    wqkv_in,
+    wproj_in,
+    wup_in,
+    wdown_in,
+    table_in,
+    pos_in,
+    mask_ref,
+    grid_ref,
+    win_in,
+    out_ref,
+    dtok_ref,
+    ggain_ref,
+    all1,
+    all2,
+    allb,
     wqkv_ref,
     wproj_ref,
     wup_ref,
     wdown_ref,
+    pos_ref,
+    win_ref,
+    load_sem,
     table_ref,
-    pos_ref,
-    mask_ref,
-    grid_ref,
-    win_ref,
-    out_ref,
-    dtok_ref,
-    ggain_ref,
-    gqkv_ref,
-    gproj_ref,
-    gup_ref,
-    gdown_ref,
-    gbias_ref,
     xs,
     xr,
     hi_ref,
@@ -160,23 +166,19 @@
     bias_ref,
     prob_ref,
     ds_ref,
-    mix_ref,
-    dpk_ref,
     pack_ref,
-    gains_ref,
+    gains_lat,
+    gains_lon,
     buf1,
     got1,
     mid1,
     gom1,
-    all1,
     buf2,
     got2,
     mid2,
     gom2,
-    all2,
     bufb,
     gotb,
-    allb,
     x_send,
     x_recv,
     lat_send,
@@ -197,6 +199,20 @@
     peers += [befores[0], afters[0]]
     for peer in peers:
         pl.semaphore_signal(barrier, inc=1, device_id=peer, device_id_type=MESH)
+
+    loads = {}
+    for k, (name, src, dst) in enumerate(
+        (
+            ("pos", pos_in, pos_ref),
+            ("win", win_in, win_ref),
+            ("qkv", wqkv_in, wqkv_ref),
+            ("proj", wproj_in, wproj_ref),
+            ("down", wdown_in, wdown_ref),
+            ("up", wup_in, wup_ref),
+        )
+    ):
+        loads[name] = pltpu.make_async_copy(src, dst, load_sem.at[k])
+        loads[name].start()
 
     def send_slots(e, devices):
         copies = []
@@ -227,6 +243,17 @@
     pl.semaphore_wait(barrier, len(peers))
     copies = send_slots(0, befores)
 
+    loads["pos"].wait()
+    loads["win"].wait()
+    for h in range(HEADS):
+        for k in range(HI_USED):
+            wide = min(LANES, NPOS - k * LANES)
+            row = pl.ds(h * HI + k, 1)
+            table_ref[row, :wide] = table_in[h, :, k * LANES : k * LANES + wide]
+        if NPOS % LANES:
+            table_ref[h * HI + HI_USED - 1 : h * HI + HI_USED, NPOS % LANES :] = jnp.zeros(
+                (1, LANES - NPOS % LANES), F32
+            )
     win = win_ref[...]
     win_rows = win[:NT]
     pos = pos_ref[...]
@@ -262,29 +289,34 @@
 
     finish(copies)
     windows = xr[0]
+    loads["qkv"].wait()
     packed = mm(windows, wqkv_ref[...]).astype(BF16)
+    query, key, value = (packed[:, part * C : (part + 1) * C] for part in range(3))
     scale = HD**-0.5
-
-    def head(h, part):
-        return packed[:, part * C + h * HD : part * C + (h + 1) * HD]
-
+    lane_head = lax.broadcasted_iota(jnp.int32, (1, C), 1) // HD
+    picks = [jnp.where(lane_head == h, 1.0, 0.0).astype(BF16) for h in range(HEADS)]
+
+    mixed = jnp.zeros((NT, C), F32)
     for h in range(HEADS):
-        scores = mm_nt(head(h, 0), head(h, 1)) * scale + bias_ref[h, :, :NT]
+        scores = mm_nt(query * picks[h], key) * scale + bias_ref[h, :, :NT]
         weight = jnp.exp(scores - jnp.max(scores, axis=-1, keepdims=True))
         prob = weight / jnp.sum(weight, axis=-1, keepdims=True)
         prob_ref[h, :, :NT] = prob
-        mix_ref[:, h * HD : (h + 1) * HD] = mm(prob.astype(BF16), head(h, 2))
-    mixture = mix_ref[...].astype(BF16)
+        mixed = mixed + mm(prob.astype(BF16), value * picks[h])
+    mixture = mixed.astype(BF16)
+    loads["proj"].wait()
     xs[1] = mm(mixture, wproj_ref[...]).astype(BF16)
     copies = send_slots(1, afters)
 
     cot = mm(grid, cot_ref[...]).astype(BF16)
-    delta_act = mm_nt(cot, wdown_ref[...])
+    loads["down"].wait()
+    delta_act = mm(cot, wdown_ref[...])
     buf1[2304:, :] = jnp.zeros((buf1.shape[0] - 2304, LANES), BF16)
     buf2[1152:, :] = jnp.zeros((buf2.shape[0] - 1152, LANES), BF16)
     bufb[...] = jnp.zeros(bufb.shape, BF16)
     ds_ref[...] = jnp.zeros(ds_ref.shape, F32)
-    gains_ref[...] = jnp.zeros(gains_ref.shape, F32)
+    gains_lat[0] = jnp.zeros((8, 256), F32)
+    loads["up"].wait()
     finish(copies)
 
     middle = (tokens + xr[1].astype(F32)).astype(BF16).astype(F32)
@@ -305,11 +337,9 @@
     grad_up = mm_tn(normed_two, delta_up).astype(BF16)
     for j in range(6):
         buf1[j * C : (j + 1) * C, :] = grad_up[:, j * LANES : (j + 1) * LANES]
-    grad_down = mm_tn(active, cot)
-    buf1[1152:1920, :] = grad_down[:, :LANES].astype(BF16)
-    pack_ref[:HID // 2, :64] = grad_down[: HID // 2, LANES:]
-    pack_ref[:HID // 2, 64:128] = grad_down[HID // 2 :, LANES:]
-    buf1[1920:2304, :] = pack_ref[: HID // 2, :LANES].astype(BF16)
+    grad_down = mm_tn(cot, active).astype(BF16)
+    for j in range(6):
+        buf1[(6 + j) * C : (7 + j) * C, :] = grad_down[:, j * LANES : (j + 1) * LANES]
 
     def exchange(axis, k):
         if axis == 0:
@@ -319,54 +349,45 @@
     rq1, rq2 = rp1 * n_lon, rp2 * n_lon
     scatter_lat1 = exchange(0, 0)
     scatter_lat1.scatter(buf1, got1, rq1)
-    output = middle + mm(active, wdown_ref[...])
+    output = middle + mm_nt(active, wdown_ref[...])
     out_ref[...] = mm_tn(grid, output.astype(BF16)).astype(BF16)
     finish(copies)
 
     delta_attn = xr[2]
     delta_mix = mm_nt(delta_attn, wproj_ref[...]).astype(BF16)
-    pack_ref[:C, 3 * C :] = mm_tn(mixture, delta_attn)
+    pack_ref[:, 3 * C :] = mm_tn(mixture, delta_attn)
+    delta_query, delta_key, delta_value = (jnp.zeros((NT, C), F32) for _ in range(3))
     for h in range(HEADS):
-        cols = slice(h * HD, (h + 1) * HD)
-        delta_head = delta_mix[:, cols]
+        delta_head = delta_mix * picks[h]
         prob = prob_ref[h, :, :NT]
-        delta_prob = mm_nt(delta_head, head(h, 2))
+        delta_prob = mm_nt(delta_head, value)
         scored = prob * (delta_prob - jnp.sum(delta_prob * prob, axis=-1, keepdims=True))
         ds_ref[h, :, :NT] = scored
         low = scored.astype(BF16)
-        dpk_ref[:, h * HD : (h + 1) * HD] = mm(low, head(h, 1)) * scale
-        dpk_ref[:, C + h * HD : C + (h + 1) * HD] = mm_tn(low, head(h, 0)) * scale
-        dpk_ref[:, 2 * C + h * HD : 2 * C + (h + 1) * HD] = mm_tn(prob.astype(BF16), delta_head)
-    delta_packed = dpk_ref[...].astype(BF16)
-    xs[3] = mm_nt(delta_packed, wqkv_ref[...]).astype(BF16)
+        delta_query = delta_query + mm(low, key * picks[h])
+        delta_key = delta_key + mm_tn(low, query * picks[h])
+        delta_value = delta_value + mm_tn(prob.astype(BF16), delta_head)
+    delta_query = (delta_query * scale).astype(BF16)
+    delta_key = (delta_key * scale).astype(BF16)
+    delta_value = delta_value.astype(BF16)
+    w_qkv = wqkv_ref[...]
+    xs[3] = (
+        mm_nt(delta_query, w_qkv[:, :C])
+        + mm_nt(delta_key, w_qkv[:, C : 2 * C])
+        + mm_nt(delta_value, w_qkv[:, 2 * C :])
+    ).astype(BF16)
     copies = send_slots(3, afters)
 
+    pack_ref[:, :C] = mm_tn(windows, delta_query)
+    pack_ref[:, C : 2 * C] = mm_tn(windows, delta_key)
+    pack_ref[:, 2 * C : 3 * C] = mm_tn(windows, delta_value)
+    for j in range(6):
+        buf2[j * C : (j + 1) * C, :] = pack_ref[:, j * LANES : (j + 1) * LANES].astype(BF16)
+    scatter_lat2 = exchange(0, 1)
+    scatter_lat2.scatter(buf2, got2, rq2)
     mid1[...] = scatter_lat1.total().astype(BF16)
     scatter_lon1 = exchange(1, 0)
     scatter_lon1.scatter(mid1, gom1, rp1)
-    pack_ref[:C, : 3 * C] = mm_tn(windows, delta_packed)
-    for j in range(6):
-        buf2[j * C : (j + 1) * C, :] = pack_ref[:C, j * LANES : (j + 1) * LANES].astype(BF16)
-    finish(copies)
-
-    delta_normed = xr[3].astype(F32)
-    delta_input, grad_gain_one = norm_back(delta_normed, normal_one, inverse_one, gain_one)
-    gains_ref[0:1, :C] = grad_gain_one
-    gains_ref[1:2, :C] = grad_gain_two
-    buf2[1152:1168, :] = gains_ref[:, :LANES].astype(BF16)
-    buf2[1168:1184, :] = gains_ref[:, LANES:].astype(BF16)
-    scatter_lat2 = exchange(0, 1)
-    scatter_lat2.scatter(buf2, got2, rq2)
-    delta_tokens = (delta_middle.astype(F32) + delta_input).astype(BF16)
-    dtok_ref[...] = mm_tn(grid, delta_tokens).astype(BF16)
-
-    def own_rows(rows):
-        return pl.multiple_of((lat * n_lon + lon) * rows, 16)
-
-    start1 = own_rows(rp1)
-    all1[pl.ds(start1, rp1), :] = (scatter_lon1.total() * factor).astype(BF16)
-    gather_lon1 = exchange(1, 1)
-    gather_lon1.gather(all1, rp1, start1)
 
     iota_hi = lax.broadcasted_iota(jnp.int32, (HI, 256), 0)
     iota_lo = lax.broadcasted_iota(jnp.int32, (LANES, 256), 0)
@@ -390,14 +411,44 @@
             )
         return acc + mm_nt(jnp.concatenate(left, axis=1), jnp.concatenate(right, axis=1))
 
-    bias_sum = lax.fori_loop(0, 20, collect, jnp.zeros((HEADS * HI, LANES), F32))
+    bias_sum = lax.fori_loop(0, 8, collect, jnp.zeros((HEADS * HI, LANES), F32))
+    finish(copies)
+
+    delta_normed = xr[3].astype(F32)
+    delta_input, grad_gain_one = norm_back(delta_normed, normal_one, inverse_one, gain_one)
+    gains_lat[0, 0:1, :C] = grad_gain_one
+    gains_lat[0, 1:2, :C] = grad_gain_two
+    gain_lat = exchange(0, 3)
+    for d in range(1, n_lat):
+        gain_lat.start(d, gains_lat.at[0], gains_lat.at[d], gain_lat.peer(d)[1])
+
+    mid2[...] = scatter_lat2.total().astype(BF16)
+    scatter_lon2 = exchange(1, 3)
+    scatter_lon2.scatter(mid2, gom2, rp2)
+
+    def own_rows(rows):
+        return pl.multiple_of((lat * n_lon + lon) * rows, 16)
+
+    start1 = own_rows(rp1)
+    all1[pl.ds(start1, rp1), :] = (scatter_lon1.total() * factor).astype(BF16)
+    gather_lon1 = exchange(1, 1)
+    gather_lon1.gather(all1, rp1, start1)
+
+    bias_sum = lax.fori_loop(8, 20, collect, bias_sum)
     bufb[: HEADS * HI, :] = bias_sum.astype(BF16)
     scatter_b = exchange(1, 2)
     scatter_b.scatter(bufb, gotb, rpb)
 
-    mid2[...] = scatter_lat2.total().astype(BF16)
-    scatter_lon2 = exchange(1, 3)
-    scatter_lon2.scatter(mid2, gom2, rp2)
+    start2 = own_rows(rp2)
+    all2[pl.ds(start2, rp2), :] = (scatter_lon2.total() * factor).astype(BF16)
+    gather_lon2 = exchange(1, 5)
+    gather_lon2.gather(all2, rp2, start2)
+
+    gain_lat.wait()
+    gains_lon[0] = jnp.sum(gains_lat[...], axis=0)
+    gain_lon = exchange(1, 6)
+    for d in range(1, n_lon):
+        gain_lon.start(d, gains_lon.at[0], gains_lon.at[d], gain_lon.peer(d)[1])
 
     gather_lon1.wait()
     gather_lat1 = exchange(0, 2)
@@ -408,30 +459,47 @@
     gather_b = exchange(1, 4)
     gather_b.gather(allb, rpb, startb)
 
-    start2 = own_rows(rp2)
-    all2[pl.ds(start2, rp2), :] = (scatter_lon2.total() * factor).astype(BF16)
-    gather_lon2 = exchange(1, 5)
-    gather_lon2.gather(all2, rp2, start2)
     gather_lon2.wait()
-    gather_lat2 = exchange(0, 3)
+    gather_lat2 = exchange(0, 4)
     gather_lat2.gather(all2, rq2, pl.multiple_of(lat * rq2, 16))
 
+    delta_tokens = (delta_middle.astype(F32) + delta_input).astype(BF16)
+    dtok_ref[...] = mm_tn(grid, delta_tokens).astype(BF16)
+    gain_lon.wait()
+    ggain_ref[...] = jnp.sum(gains_lon[...], axis=0) * factor
     gather_b.wait()
-    gbias_ref[...] = allb[: HEADS * HI, :].astype(F32)
     gather_lat1.wait()
+    gather_lat2.wait()
+
+
+def unpack(
+    ggain_in,
+    all1,
+    all2,
+    allb,
+    gain1_ref,
+    gain2_ref,
+    gqkv_ref,
+    gproj_ref,
+    gup_ref,
+    gdown_ref,
+    gbias_ref,
+    pack_ref,
+):
+    gain1_ref[...] = ggain_in[0:1, :C]
+    gain2_ref[...] = ggain_in[1:2, :C]
     for j in range(6):
-        gup_ref[:, j * LANES : (j + 1) * LANES] = all1[j * C : (j + 1) * C, :].astype(F32)
-    gdown_ref[:, :LANES] = all1[1152:1920, :].astype(F32)
-    tail = all1[1920:2304, :].astype(F32)
-    gdown_ref[: HID // 2, LANES:] = tail[:, :64]
-    gdown_ref[HID // 2 :, LANES:] = tail[:, 64:]
-    gather_lat2.wait()
-    for j in range(6):
-        pack_ref[:C, j * LANES : (j + 1) * LANES] = all2[j * C : (j + 1) * C, :].astype(F32)
-    gqkv_ref[...] = pack_ref[:C, : 3 * C]
-    gproj_ref[...] = pack_ref[:C, 3 * C :]
-    ggain_ref[:, :LANES] = all2[1152:1168, :].astype(F32)
-    ggain_ref[:, LANES:] = all2[1168:1184, :].astype(F32)
+        cols = slice(j * LANES, (j + 1) * LANES)
+        gup_ref[:, cols] = all1[j * C : (j + 1) * C, :].astype(F32)
+        gdown_ref[:, cols] = all1[(6 + j) * C : (7 + j) * C, :].astype(F32)
+        pack_ref[:, cols] = all2[j * C : (j + 1) * C, :].astype(F32)
+    gqkv_ref[...] = pack_ref[:, : 3 * C]
+    gproj_ref[...] = pack_ref[:, 3 * C :]
+    for h in range(HEADS):
+        rows = allb[h * HI : (h + 1) * HI, :].astype(F32)
+        for k in range(HI_USED):
+            wide = min(LANES, NPOS - k * LANES)
+            gbias_ref[h, :, k * LANES : k * LANES + wide] = rows[k : k + 1, :wide]
 
 
 def up_to(value, unit):
@@ -456,10 +524,9 @@
     n = n_lat * n_lon
     factor = 1.0 / math.sqrt(WT * n)
     rp1 = up_to(-(-2304 // n), 16)
-    rp2 = up_to(-(-1184 // n), 16)
+    rp2 = up_to(-(-1152 // n), 16)
     rpb = up_to(-(-HEADS * HI // n_lon), 16)
     grid, window = orders()
-    table = jnp.pad(bias_table.reshape(HEADS, NPOS), ((0, 0), (0, HI * LANES - NPOS)))
     args = (
         tokens.reshape(WT, C),
         cotangent.reshape(WT, C),
@@ -468,8 +535,8 @@
         qkv_weight,
         proj_weight,
         up_weight,
-        down_weight,
-        table.reshape(HEADS * HI, LANES),
+        down_weight.T,
+        bias_table.reshape(HEADS, 1, NPOS),
         pos_index,
         mask_ids.reshape(1, WT),
         jnp.asarray(grid, BF16),
@@ -479,12 +546,10 @@
     outs = (
         shape((WT, C), BF16),
         shape((WT, C), BF16),
-        shape((16, 256), F32),
-        shape((C, 3 * C), F32),
-        shape((C, C), F32),
-        shape((C, HID), F32),
-        shape((HID, C), F32),
-        shape((HEADS * HI, LANES), F32),
+        shape((8, 256), F32),
+        shape((rp1 * n, LANES), BF16),
+        shape((rp2 * n, LANES), BF16),
+        shape((rpb * n_lon, LANES), BF16),
     )
 
     def rows(count):
@@ -492,6 +557,14 @@
 
     dma = pltpu.SemaphoreType.DMA
     scratch = [
+        pltpu.VMEM((C, 3 * C), BF16),
+        pltpu.VMEM((C, C), BF16),
+        pltpu.VMEM((C, HID), BF16),
+        pltpu.VMEM((C, HID), BF16),
+        pltpu.VMEM((WT, WT), jnp.int32),
+        pltpu.VMEM((256, WT), BF16),
+        dma((6,)),
+        pltpu.VMEM((HEADS * HI, LANES), F32),
         pltpu.VMEM((4, NT, C), BF16),
         pltpu.VMEM((4, NT, C), BF16),
         pltpu.VMEM((NT, 256), jnp.int32),
@@ -499,10 +572,9 @@
         pltpu.VMEM((HEADS, NT, 256), F32),
         pltpu.VMEM((HEADS, NT, 256), F32),
         pltpu.VMEM((HEADS, NT, 256), F32),
-        pltpu.VMEM((NT, C), F32),
-        pltpu.VMEM((NT, 3 * C), F32),
-        pltpu.VMEM((HID // 2, HID), F32),
-        pltpu.VMEM((16, 256), F32),
+        pltpu.VMEM((C, HID), F32),
+        pltpu.VMEM((n_lat, 8, 256), F32),
+        pltpu.VMEM((n_lon, 8, 256), F32),
     ]
     for rp in (rp1, rp2):
         scratch += [
@@ -510,38 +582,56 @@
             rows(rp * n_lon * (n_lat - 1)),
             rows(rp * n_lon),
             rows(rp * (n_lon - 1)),
-            rows(rp * n),
         ]
-    scratch += [rows(rpb * n_lon), rows(rpb * (n_lon - 1)), rows(rpb * n_lon)]
+    scratch += [rows(rpb * n_lon), rows(rpb * (n_lon - 1))]
     scratch += [
         dma((4, 3)),
         dma((4, 3)),
-        dma((4, n_lat - 1)),
-        dma((4, n_lat - 1)),
-        dma((6, n_lon - 1)),
-        dma((6, n_lon - 1)),
+        dma((5, n_lat - 1)),
+        dma((5, n_lat - 1)),
+        dma((7, n_lon - 1)),
+        dma((7, n_lon - 1)),
     ]
     vmem = pl.BlockSpec(memory_space=pltpu.VMEM)
-    out, dtok, ggain, gqkv, gproj, gup, gdown, gbias = pl.pallas_call(
+    hbm = pl.BlockSpec(memory_space=pltpu.HBM)
+    in_specs = [vmem] * 4 + [hbm] * 4 + [vmem, hbm, vmem, vmem, hbm]
+    out, dtok, *sums = pl.pallas_call(
         functools.partial(kernel, n_lat, n_lon, factor, rp1, rp2, rpb),
         out_shape=outs,
-        in_specs=[vmem] * len(args),
+        in_specs=in_specs,
         out_specs=[vmem] * len(outs),
         scratch_shapes=scratch,
         compiler_params=pltpu.CompilerParams(
             collective_id=0, has_side_effects=True, vmem_limit_bytes=48 * 1024 * 1024
         ),
     )(*args)
+    results = (
+        shape((1, C), F32),
+        shape((1, C), F32),
+        shape((C, 3 * C), F32),
+        shape((C, C), F32),
+        shape((C, HID), F32),
+        shape((C, HID), F32),
+        shape((HEADS, 1, NPOS), F32),
+    )
+    gain1, gain2, gqkv, gproj, gup, gdown, gbias = pl.pallas_call(
+        unpack,
+        out_shape=results,
+        in_specs=[vmem] * len(sums),
+        out_specs=[vmem] * len(results),
+        scratch_shapes=[pltpu.VMEM((C, HID), F32)],
+        compiler_params=pltpu.CompilerParams(vmem_limit_bytes=32 * 1024 * 1024),
+    )(*sums)
     return (
         out.reshape(tokens.shape),
         dtok.reshape(tokens.shape),
-        ggain[0, :C],
-        ggain[1, :C],
+        gain1.reshape(C),
+        gain2.reshape(C),
         gqkv,
         gproj,
         gup,
-        gdown,
-        gbias.reshape(HEADS, HI * LANES)[:, :NPOS].reshape(bias_table.shape),
+        gdown.T,
+        gbias.reshape(bias_table.shape),
     )
 
 

time: 81.4 us -> 70.1 us (0.86)
  local copies, waits for them, and re-layouts: 16.5 us -> 9.57 us
  Pallas kernels: 63.6 us -> 59.4 us
    pallas_call x1, Pallas kernels: 63.6 us -> 58.1 us  [local(): pl.pallas_call(functools.partial(kernel, n_lat, n_lon, factor, rp1, rp2,...]
    unnamed x43 -> x27, local copies, waits for them, and re-layouts: 14 us -> 9.35 us
    pallas_call x0 -> x1, Pallas kernels: none -> 1.32 us  [local(): pl.pallas_call(unpack, out_shape=results, in_specs=[vmem] * len(sums), ou...]
    reshape x1, local copies, waits for them, and re-layouts: 0.91 us -> 0.03 us  [local(): out.reshape(tokens.shape)]
where the time goes in v2:
time: 70.1 us; the launch traced here: 69.7 us
  Pallas kernels  59.4 us (85%)
  local copies, waits for them, and re-layouts  9.57 us (14%)
  between operations  0.73 us (1%)
    pallas_call x1, Pallas kernels, local(): pl.pallas_call(functools.partial(kernel, n_lat, n_lon, factor, rp1, rp2,...  58.1 us
    unnamed x27, local copies, waits for them, and re-layouts  9.35 us

profile of v2, /device:TPU:1, one launch (start us, length us, event | category | flops | bytes accessed | tf_op | source)
XLA Modules:
  0.0 69.7 jit_solution(9925839384227306055)
XLA Ops:
  0.6 0.0 copy-start.10
  0.7 0.7 copy-done.10
  1.3 0.0 copy-start.8
  1.3 0.0 copy-start.9
  1.3 0.1 reshape.56.mask_ref
  1.4 0.0 copy-start.1
  1.4 0.9 %copy.28 = bf16[2,6,12,192]{3,2,1,0:T(8,128)(2,1)S(1)} copy(bf16[2,6,12,192]{3,0,2,1:T(2,128)(2,1)} %param.13) | data formatting | bytes 110592 | tf_op args[0]
  2.4 0.0 copy-start
  2.4 0.9 %copy.29 = bf16[2,6,12,192]{3,2,1,0:T(8,128)(2,1)S(1)} copy(bf16[2,6,12,192]{3,0,2,1:T(2,128)(2,1)} %param.23) | data formatting | bytes 110592 | tf_op args[10]
  3.4 0.0 copy-start.5
  3.4 0.0 copy-done.8
  3.4 0.0 copy-done.9
  3.4 0.0 copy-done.1
  3.5 0.0 copy-done
  3.5 0.8 %copy-done.5 = bf16[192,192]{1,0:T(8,128)(2,1)S(1)} copy-done((bf16[192,192]{1,0:T(8,128)(2,1)S(1)}, bf16[192,192]{1,0:T(8,128)(2,1)}, u32[]{:S(2)}) %copy-start.5) | copy-done | bytes 73752
  4.3 0.0 copy-start.2
  4.3 0.9 %copy-done.2 = bf16[192,576]{1,0:T(8,128)(2,1)S(1)} copy-done((bf16[192,576]{1,0:T(8,128)(2,1)S(1)}, bf16[192,576]{1,0:T(8,128)(2,1)}, u32[]{:S(2)}) %copy-start.2) | copy-done | bytes 221208
  5.2 0.0 copy-start.3
  5.2 0.9 %copy-done.3 = s32[144,144]{1,0:T(8,128)S(1)} copy-done((s32[144,144]{1,0:T(8,128)S(1)}, s32[144,144]{1,0:T(8,128)}, u32[]{:S(2)}) %copy-start.3) | copy-done | bytes 82968
  6.1 0.0 copy-start.4
  6.1 0.9 %copy-done.4 = bf16[256,144]{1,0:T(8,128)(2,1)S(1)} copy-done((bf16[256,144]{1,0:T(8,128)(2,1)S(1)}, bf16[256,144]{1,0:T(8,128)(2,1)}, u32[]{:S(2)}) %copy-start.4) | copy-done | bytes 73752
  7.0 0.0 copy-start.6
  7.0 0.9 %copy-done.6 = bf16[192,144]{1,0:T(8,128)(2,1)S(1)} copy-done((bf16[192,144]{1,0:T(8,128)(2,1)S(1)}, bf16[192,144]{1,0:T(8,128)(2,1)}, u32[]{:S(2)}) %copy-start.6) | copy-done | bytes 55320
  7.9 0.0 copy-start.7
  7.9 0.9 %copy-done.7 = f32[6,1,1,3312]{3,2,1,0:T(1,128)S(1)} copy-done((f32[6,1,1,3312]{3,2,1,0:T(1,128)S(1)}, f32[6,1,1,3312]{3,2,1,0:T(1,128)}, u32[]{:S(2)}) %copy-start.7) | copy-done | bytes 79512
  8.8 58.1 %shard_map.196 = (bf16[144,192]{1,0:T(8,128)(2,1)S(1)}, bf16[144,192]{1,0:T(8,128)(2,1)S(1)}, f32[8,256]{1,0:T(8,128)S(1)}, bf16[2560,128]{1,0:T(8,128)(2,1)S(1)...) custom-call(bf16[144,192]{1,0:T(8,128)(2,1)S(1)} %reshape.51.tokens_ref, ...), custom_call_target="tpu_custom_call" | custom-call | tf_op jit(solution)/shard_map/pallas_call | solution.py:598
  67.0 0.7 %copy.31 = bf16[2,6,12,192]{3,0,2,1:T(2,128)(2,1)} copy(bf16[2,6,12,192]{3,2,1,0:T(8,128)(2,1)S(1)} %reshape.57) | data formatting | bytes 110592
  67.7 0.7 %copy.32 = bf16[2,6,12,192]{3,0,2,1:T(2,128)(2,1)} copy(bf16[2,6,12,192]{3,2,1,0:T(8,128)(2,1)S(1)} %reshape.58) | data formatting | bytes 110592
  68.4 1.3 %shard_map.197 = (f32[1,192]{1,0:T(1,128)}, f32[1,192]{1,0:T(1,128)}, f32[192,576]{1,0:T(8,128)}, f32[192,192]{1,0:T(8,128)}, f32[192,768]{1,0:T(8,128)}, /*index=5*/f32[192,768]{1,0:T(8,128)}, f32[6,1,3312]{2,1,0:T(1,128)}) custom-call(f32[8,256]{1,0:T(8,128)S(1)} %get-tuple-element.24.ggain_in, bf16[2560,128]{1,0:T(8,128)(2,1)S(1)} %get-tuple-element.25.all1, ...), custom_call_target="tpu_custom_call" | custom-call | tf_op jit(solution)/shard_map/pallas_call | solution.py:617
  (5 shorter events, 0.1 us)
Async XLA Ops:
  0.6 0.7 copy-start.10
  1.3 2.1 %copy-start.8 = (f32[192]{0:T(256)S(1)}, f32[192]{0:T(256)}, u32[]{:S(2)}) copy-start(f32[192]{0:T(256)} %param.14) | copy-start | bytes 2308
  1.3 2.1 %copy-start.9 = (f32[192]{0:T(256)S(1)}, f32[192]{0:T(256)}, u32[]{:S(2)}) copy-start(f32[192]{0:T(256)} %param.15) | copy-start | bytes 2308
  1.4 2.0 %copy-start.1 = (bf16[768,192]{0,1:T(8,128)(2,1)S(1)}, bf16[768,192]{0,1:T(8,128)(2,1)}, u32[]{:S(2)}) copy-start(bf16[768,192]{0,1:T(8,128)(2,1)} %param.19) | copy-start | bytes 884740
  2.4 1.1 %copy-start = (bf16[192,768]{1,0:T(8,128)(2,1)S(1)}, bf16[192,768]{1,0:T(8,128)(2,1)}, u32[]{:S(2)}) copy-start(bf16[192,768]{1,0:T(8,128)(2,1)} %wup_in.1) | copy-start | bytes 884740
  3.4 0.9 %copy-start.5 = (bf16[192,192]{1,0:T(8,128)(2,1)S(1)}, bf16[192,192]{1,0:T(8,128)(2,1)}, u32[]{:S(2)}) copy-start(bf16[192,192]{1,0:T(8,128)(2,1)} %wproj_in.1) | copy-start | bytes 221188
  4.3 0.9 %copy-start.2 = (bf16[192,576]{1,0:T(8,128)(2,1)S(1)}, bf16[192,576]{1,0:T(8,128)(2,1)}, u32[]{:S(2)}) copy-start(bf16[192,576]{1,0:T(8,128)(2,1)} %wqkv_in.1) | copy-start | bytes 663556
  5.2 0.9 %copy-start.3 = (s32[144,144]{1,0:T(8,128)S(1)}, s32[144,144]{1,0:T(8,128)}, u32[]{:S(2)}) copy-start(s32[144,144]{1,0:T(8,128)} %pos_in.1) | copy-start | bytes 248836
  6.1 0.9 %copy-start.4 = (bf16[256,144]{1,0:T(8,128)(2,1)S(1)}, bf16[256,144]{1,0:T(8,128)(2,1)}, u32[]{:S(2)}) copy-start(bf16[256,144]{1,0:T(8,128)(2,1)} %constant.5.clone.win_in) | copy-start | bytes 221188
  7.0 0.9 %copy-start.6 = (bf16[192,144]{1,0:T(8,128)(2,1)S(1)}, bf16[192,144]{1,0:T(8,128)(2,1)}, u32[]{:S(2)}) copy-start(bf16[192,144]{1,0:T(8,128)(2,1)} %constant.4.clone.grid_ref) | copy-start | bytes 165892
  7.9 0.9 %copy-start.7 = (f32[6,1,1,3312]{3,2,1,0:T(1,128)S(1)}, f32[6,1,1,3312]{3,2,1,0:T(1,128)}, u32[]{:S(2)}) copy-start(f32[6,1,1,3312]{3,2,1,0:T(1,128)} %param.20) | copy-start | bytes 238468

commit v3 on v2

--- a/solution.py
+++ b/solution.py
@@ -3,7 +3,6 @@
 
 import jax
 import jax.numpy as jnp
-import numpy as np
 from jax import lax
 from jax.experimental import pallas as pl
 from jax.experimental.pallas import tpu as pltpu
@@ -29,18 +28,21 @@
 MESH = pl.DeviceIdType.MESH
 
 
-def orders():
-    grid = np.zeros((NT, WT), np.float32)
-    window = np.zeros((256, WT), np.float32)
-    for rh in range(2):
-        for ch in range(2):
-            for z in range(2):
-                for r in range(3):
-                    for c in range(6):
-                        row = (rh * 2 + ch) * SLOT + z * 18 + r * 6 + c
-                        grid[row, z * 72 + (3 * rh + r) * 12 + 6 * ch + c] = 1
-                        window[row, (1 - z) * 72 + (3 * (1 - rh) + r) * 12 + 6 * (1 - ch) + c] = 1
-    return grid, window
+def order(rows, window):
+    row = lax.broadcasted_iota(jnp.int32, (rows, 1), 0)
+    slot = (row * 171) >> 13
+    rest = row - slot * SLOT
+    z = (rest * 57) >> 10
+    inner = rest - z * 18
+    r = (inner * 43) >> 8
+    c = inner - r * 6
+    rh, ch = slot >> 1, slot & 1
+    if window:
+        z, rh, ch = 1 - z, 1 - rh, 1 - ch
+    token = z * 72 + (3 * rh + r) * 12 + 6 * ch + c
+    token = jnp.where((rest < 36) & (slot < 4), token, -1)
+    lane = lax.broadcasted_iota(jnp.int32, (rows, WT), 1)
+    return jnp.where(lane == token, 1.0, 0.0).astype(BF16)
 
 
 def mm(a, b):
@@ -143,8 +145,6 @@
     table_in,
     pos_in,
     mask_ref,
-    grid_ref,
-    win_in,
     out_ref,
     dtok_ref,
     ggain_ref,
@@ -156,7 +156,6 @@
     wup_ref,
     wdown_ref,
     pos_ref,
-    win_ref,
     load_sem,
     table_ref,
     xs,
@@ -204,7 +203,6 @@
     for k, (name, src, dst) in enumerate(
         (
             ("pos", pos_in, pos_ref),
-            ("win", win_in, win_ref),
             ("qkv", wqkv_in, wqkv_ref),
             ("proj", wproj_in, wproj_ref),
             ("down", wdown_in, wdown_ref),
@@ -235,7 +233,7 @@
         for copy in copies:
             copy.wait()
 
-    grid = grid_ref[...]
+    grid = order(NT, False)
     tokens = mm(grid, tokens_ref[...])
     normal_one, inverse_one = norm_stats(tokens)
     gain_one = gain1_ref[...]
@@ -244,7 +242,6 @@
     copies = send_slots(0, befores)
 
     loads["pos"].wait()
-    loads["win"].wait()
     for h in range(HEADS):
         for k in range(HI_USED):
             wide = min(LANES, NPOS - k * LANES)
@@ -254,7 +251,7 @@
             table_ref[h * HI + HI_USED - 1 : h * HI + HI_USED, NPOS % LANES :] = jnp.zeros(
                 (1, LANES - NPOS % LANES), F32
             )
-    win = win_ref[...]
+    win = order(256, True)
     win_rows = win[:NT]
     pos = pos_ref[...]
     hi = (pos >> 7).astype(F32).astype(BF16)
@@ -526,7 +523,6 @@
     rp1 = up_to(-(-2304 // n), 16)
     rp2 = up_to(-(-1152 // n), 16)
     rpb = up_to(-(-HEADS * HI // n_lon), 16)
-    grid, window = orders()
     args = (
         tokens.reshape(WT, C),
         cotangent.reshape(WT, C),
@@ -539,8 +535,6 @@
         bias_table.reshape(HEADS, 1, NPOS),
         pos_index,
         mask_ids.reshape(1, WT),
-        jnp.asarray(grid, BF16),
-        jnp.asarray(window, BF16),
     )
     shape = jax.ShapeDtypeStruct
     outs = (
@@ -562,8 +556,7 @@
         pltpu.VMEM((C, HID), BF16),
         pltpu.VMEM((C, HID), BF16),
         pltpu.VMEM((WT, WT), jnp.int32),
-        pltpu.VMEM((256, WT), BF16),
-        dma((6,)),
+        dma((5,)),
         pltpu.VMEM((HEADS * HI, LANES), F32),
         pltpu.VMEM((4, NT, C), BF16),
         pltpu.VMEM((4, NT, C), BF16),
@@ -594,7 +587,7 @@
     ]
     vmem = pl.BlockSpec(memory_space=pltpu.VMEM)
     hbm = pl.BlockSpec(memory_space=pltpu.HBM)
-    in_specs = [vmem] * 4 + [hbm] * 4 + [vmem, hbm, vmem, vmem, hbm]
+    in_specs = [vmem] * 4 + [hbm] * 4 + [vmem, hbm, vmem]
     out, dtok, *sums = pl.pallas_call(
         functools.partial(kernel, n_lat, n_lon, factor, rp1, rp2, rpb),
         out_shape=outs,

time: 70.1 us -> 68.3 us (0.974)
  local copies, waits for them, and re-layouts: 9.57 us -> 7.77 us
    unnamed x27 -> x23, local copies, waits for them, and re-layouts: 9.35 us -> 7.56 us
where the time goes in v3:
time: 68.3 us; the launch traced here: 68 us
  Pallas kernels  59.5 us (87%)
  local copies, waits for them, and re-layouts  7.77 us (11%)
  between operations  0.73 us (1%)
    pallas_call x1, Pallas kernels, local(): pl.pallas_call(functools.partial(kernel, n_lat, n_lon, factor, rp1, rp2,...  58.1 us
    unnamed x23, local copies, waits for them, and re-layouts  7.56 us

profile of v3, /device:TPU:1, one launch (start us, length us, event | category | flops | bytes accessed | tf_op | source)
XLA Modules:
  0.0 68.0 jit_solution(6406067434080522962)
XLA Ops:
  0.6 0.0 copy-start.8
  0.7 0.7 %copy-done.8 = s32[2,6,12]{2,0,1:T(2,128)S(1)} copy-done((s32[2,6,12]{2,0,1:T(2,128)S(1)}, s32[2,6,12]{2,0,1:T(2,128)}, u32[]{:S(2)}) %copy-start.8) | copy-done | bytes 600
  1.3 0.0 copy-start.6
  1.3 0.0 copy-start.7
  1.3 0.1 reshape.56.mask_ref
  1.4 0.0 copy-start.1
  1.4 0.9 %copy.26 = bf16[2,6,12,192]{3,2,1,0:T(8,128)(2,1)S(1)} copy(bf16[2,6,12,192]{3,0,2,1:T(2,128)(2,1)} %param.11) | data formatting | bytes 110592 | tf_op args[0]
  2.4 0.0 copy-start
  2.4 0.9 %copy.27 = bf16[2,6,12,192]{3,2,1,0:T(8,128)(2,1)S(1)} copy(bf16[2,6,12,192]{3,0,2,1:T(2,128)(2,1)} %param.21) | data formatting | bytes 110592 | tf_op args[10]
  3.4 0.0 copy-start.4
  3.4 0.0 copy-done.6
  3.4 0.0 copy-done.7
  3.4 0.0 copy-done.1
  3.5 0.0 copy-done
  3.5 0.8 %copy-done.4 = bf16[192,192]{1,0:T(8,128)(2,1)S(1)} copy-done((bf16[192,192]{1,0:T(8,128)(2,1)S(1)}, bf16[192,192]{1,0:T(8,128)(2,1)}, u32[]{:S(2)}) %copy-start.4) | copy-done | bytes 73752
  4.3 0.0 copy-start.2
  4.3 0.9 %copy-done.2 = bf16[192,576]{1,0:T(8,128)(2,1)S(1)} copy-done((bf16[192,576]{1,0:T(8,128)(2,1)S(1)}, bf16[192,576]{1,0:T(8,128)(2,1)}, u32[]{:S(2)}) %copy-start.2) | copy-done | bytes 221208
  5.2 0.0 copy-start.3
  5.2 0.9 %copy-done.3 = s32[144,144]{1,0:T(8,128)S(1)} copy-done((s32[144,144]{1,0:T(8,128)S(1)}, s32[144,144]{1,0:T(8,128)}, u32[]{:S(2)}) %copy-start.3) | copy-done | bytes 82968
  6.1 0.0 copy-start.5
  6.1 0.9 %copy-done.5 = f32[6,1,1,3312]{3,2,1,0:T(1,128)S(1)} copy-done((f32[6,1,1,3312]{3,2,1,0:T(1,128)S(1)}, f32[6,1,1,3312]{3,2,1,0:T(1,128)}, u32[]{:S(2)}) %copy-start.5) | copy-done | bytes 79512
  7.0 58.1 %shard_map.178 = (bf16[144,192]{1,0:T(8,128)(2,1)S(1)}, bf16[144,192]{1,0:T(8,128)(2,1)S(1)}, f32[8,256]{1,0:T(8,128)S(1)}, bf16[2560,128]{1,0:T(8,128)(2,1)S(1)...) custom-call(bf16[144,192]{1,0:T(8,128)(2,1)S(1)} %reshape.51.tokens_ref, ...), custom_call_target="tpu_custom_call" | custom-call | tf_op jit(solution)/shard_map/pallas_call | solution.py:591
  65.2 0.7 %copy.29 = bf16[2,6,12,192]{3,0,2,1:T(2,128)(2,1)} copy(bf16[2,6,12,192]{3,2,1,0:T(8,128)(2,1)S(1)} %reshape.57) | data formatting | bytes 110592
  65.9 0.7 %copy.30 = bf16[2,6,12,192]{3,0,2,1:T(2,128)(2,1)} copy(bf16[2,6,12,192]{3,2,1,0:T(8,128)(2,1)S(1)} %reshape.58) | data formatting | bytes 110592
  66.6 1.3 %shard_map.179 = (f32[1,192]{1,0:T(1,128)}, f32[1,192]{1,0:T(1,128)}, f32[192,576]{1,0:T(8,128)}, f32[192,192]{1,0:T(8,128)}, f32[192,768]{1,0:T(8,128)}, /*index=5*/f32[192,768]{1,0:T(8,128)}, f32[6,1,3312]{2,1,0:T(1,128)}) custom-call(f32[8,256]{1,0:T(8,128)S(1)} %get-tuple-element.24.ggain_in, bf16[2560,128]{1,0:T(8,128)(2,1)S(1)} %get-tuple-element.25.all1, ...), custom_call_target="tpu_custom_call" | custom-call | tf_op jit(solution)/shard_map/pallas_call | solution.py:610
  (5 shorter events, 0.1 us)
Async XLA Ops:
  0.6 0.7 %copy-start.8 = (s32[2,6,12]{2,0,1:T(2,128)S(1)}, s32[2,6,12]{2,0,1:T(2,128)}, u32[]{:S(2)}) copy-start(s32[2,6,12]{2,0,1:T(2,128)} %param.20) | copy-start | bytes 1732
  1.3 2.1 %copy-start.6 = (f32[192]{0:T(256)S(1)}, f32[192]{0:T(256)}, u32[]{:S(2)}) copy-start(f32[192]{0:T(256)} %param.12) | copy-start | bytes 2308
  1.3 2.1 %copy-start.7 = (f32[192]{0:T(256)S(1)}, f32[192]{0:T(256)}, u32[]{:S(2)}) copy-start(f32[192]{0:T(256)} %param.13) | copy-start | bytes 2308
  1.4 2.0 %copy-start.1 = (bf16[768,192]{0,1:T(8,128)(2,1)S(1)}, bf16[768,192]{0,1:T(8,128)(2,1)}, u32[]{:S(2)}) copy-start(bf16[768,192]{0,1:T(8,128)(2,1)} %param.17) | copy-start | bytes 884740
  2.4 1.1 %copy-start = (bf16[192,768]{1,0:T(8,128)(2,1)S(1)}, bf16[192,768]{1,0:T(8,128)(2,1)}, u32[]{:S(2)}) copy-start(bf16[192,768]{1,0:T(8,128)(2,1)} %wup_in.1) | copy-start | bytes 884740
  3.4 0.9 %copy-start.4 = (bf16[192,192]{1,0:T(8,128)(2,1)S(1)}, bf16[192,192]{1,0:T(8,128)(2,1)}, u32[]{:S(2)}) copy-start(bf16[192,192]{1,0:T(8,128)(2,1)} %wproj_in.1) | copy-start | bytes 221188
  4.3 0.9 %copy-start.2 = (bf16[192,576]{1,0:T(8,128)(2,1)S(1)}, bf16[192,576]{1,0:T(8,128)(2,1)}, u32[]{:S(2)}) copy-start(bf16[192,576]{1,0:T(8,128)(2,1)} %wqkv_in.1) | copy-start | bytes 663556
  5.2 0.9 %copy-start.3 = (s32[144,144]{1,0:T(8,128)S(1)}, s32[144,144]{1,0:T(8,128)}, u32[]{:S(2)}) copy-start(s32[144,144]{1,0:T(8,128)} %pos_in.1) | copy-start | bytes 248836
  6.1 0.9 %copy-start.5 = (f32[6,1,1,3312]{3,2,1,0:T(1,128)S(1)}, f32[6,1,1,3312]{3,2,1,0:T(1,128)}, u32[]{:S(2)}) copy-start(f32[6,1,1,3312]{3,2,1,0:T(1,128)} %param.18) | copy-start | bytes 238468
